TPU v7x, 32 devices: a whole 2x2x4 slice. The times are simulated.
32 devices in a mesh: groups: 2 (over x), brick: 16 (over z, y, core).
Axes of the slice: x: 2, y: 2, z: 4, core: 2. Of those that a mesh axis runs over, the one named last changes fastest.
Arguments:
- point_features: bfloat16 [32, 131072], P(None, ('groups', 'brick')), parts along dimension 1, may hold values from -6 to 6
- point_positions: float32 [3, 131072], P(None, ('groups', 'brick')), parts along dimension 1, may hold values from -1 to 128, as said below
- owner_brick: int32 [1024], P(('groups', 'brick')), parts along dimension 0, may hold values from 0 to 15, as said below
- block_rows: int32 [1024, 4], P(('groups', 'brick')), parts along dimension 0, may hold values from 0 to 1023, as said below
- mode_scale: float32 [32, 32, 32, 64], P(None, None, 'brick'), may hold values from -8 to 8
- channel_mix: float32 [32, 32], replicated, may hold values from -1 to 1
- skip_weight: bfloat16 [32, 32], replicated, may hold values from -1 to 1
- cotangent: bfloat16 [32, 256, 128, 128], P(None, ('groups', 'brick')), parts along dimension 1, may hold values from -6 to 6
Outputs:
- latent_grid: bfloat16 [32, 256, 128, 128], P(None, ('groups', 'brick')), parts along dimension 1
- point_grads: bfloat16 [32, 131072], P(None, ('groups', 'brick')), parts along dimension 1
- mix_grads: float32 [64, 32], P('groups'), parts along dimension 0
There are 2 independent parts, one for each index of `groups`. A program takes and returns all parts, laid end to end along the dimension named above; an argument that names none is the same for every part. Nothing has to cross between parts.
Inputs may be any that keep to these rules, and one draw needn't show every extreme that they name: `owner_brick`: of the 32 blocks of one brick's points, at most 6 share an owner; in every draw one brick owns exactly 6 blocks of every brick's points. `block_rows`: row = plane * 128 + y inside the owner's slab; a block's 4 rows share the plane and have consecutive y. `point_positions`: dimension 0 holds x, y, z. A block's points lie within half a cell in x of its rows' plane and within half a cell in y of its rows' span.
All inputs are finite; a program needn't handle non-finite values.
Results may differ from a plain program's by a relative error of at most 0.015.
Values may be sent and summed in bfloat16 or wider, within the bound.
A program may use at most 192 MiB of HBM per device.

v0:
```python
import math

import jax
import jax.numpy as jnp
from jax import lax
from jax.sharding import PartitionSpec as P


def spectral_tables(grid_size, mode_count):
    positions = jnp.arange(grid_size, dtype=jnp.int32)
    numbers = jnp.arange(mode_count, dtype=jnp.int32)
    signed = jnp.where(numbers < mode_count // 2, numbers, numbers - mode_count)
    multiple = positions[:, None] * signed[None, :] % grid_size
    angles = multiple.astype(jnp.float32) * (2.0 * math.pi / grid_size)
    cosine_table = jnp.cos(angles).astype(jnp.bfloat16)
    sine_table = jnp.sin(angles).astype(jnp.bfloat16)
    line_turns = positions[:, None] * numbers[None, :] % grid_size
    line_angles = line_turns.astype(jnp.float32) * (2.0 * math.pi / grid_size)
    line_table = jnp.stack([jnp.cos(line_angles), -jnp.sin(line_angles)], axis=-1)
    line_table = line_table.reshape(grid_size, 2 * mode_count).astype(jnp.bfloat16)
    return (cosine_table, sine_table, line_table)


def rotate(values, direction):
    paired = values.reshape(values.shape[:-1] + (values.shape[-1] // 2, 2))
    turned = jnp.stack([direction * paired[..., 1], -direction * paired[..., 0]], axis=-1)
    return turned.reshape(values.shape)


def fourier_section(pattern, values, cosine_table, sine_table, direction):
    direct = jnp.einsum(pattern, values, cosine_table, preferred_element_type=jnp.float32)
    turned = jnp.einsum(pattern, values, sine_table, preferred_element_type=jnp.float32)
    return direct + rotate(turned, direction)


def complex_times(factor, values, conjugate):
    factor_pairs = factor.reshape(factor.shape[:-1] + (-1, 2))
    value_pairs = values.reshape(values.shape[:-1] + (-1, 2))
    factor_re = factor_pairs[..., 0]
    factor_im = factor_pairs[..., 1]
    value_re = value_pairs[..., 0]
    value_im = value_pairs[..., 1]
    if conjugate:
        real_part = factor_re * value_re + factor_im * value_im
        imag_part = factor_re * value_im - factor_im * value_re
    else:
        real_part = factor_re * value_re - factor_im * value_im
        imag_part = factor_re * value_im + factor_im * value_re
    return jnp.stack([real_part, imag_part], axis=-1).reshape(values.shape)


def kernels(places, row_across, row_along, grid_size):
    near_plane = jnp.exp(
        -0.5
        * (
            (row_across[:, :, None] - places[0][:, None, :]) ** 2
            + (row_along[:, :, None] - places[1][:, None, :]) ** 2
        )
    )
    depths = jnp.arange(grid_size, dtype=jnp.float32)
    near_line = jnp.exp(-0.5 * (depths[None, :, None] - places[2][:, None, :]) ** 2).astype(
        jnp.bfloat16
    )
    return (near_plane, near_line)


def contribute(block_features, near_plane, near_line):
    weighted = (block_features[:, :, None, :] * near_plane[None]).astype(jnp.bfloat16)
    return jnp.einsum("csjp,szp->csjz", weighted, near_line, preferred_element_type=jnp.float32)


def pull_back(rows_grad, near_plane, near_line):
    grad_near = jnp.einsum(
        "csjz,szp->csjp", rows_grad, near_line, preferred_element_type=jnp.float32
    )
    return jnp.sum(grad_near * near_plane[None], axis=2)


def into_modes(values):
    return lax.all_to_all(values, "brick", split_axis=2, concat_axis=1, tiled=True)


def into_slabs(values):
    return lax.all_to_all(values, "brick", split_axis=1, concat_axis=2, tiled=True)


def shards(
    point_features,
    point_positions,
    owner_brick,
    block_rows,
    mode_scale,
    channel_mix,
    skip_weight,
    cotangent,
):
    channels, points = point_features.shape
    blocks = points // 128
    pair_count = block_rows.shape[1]
    slab_planes = cotangent.shape[1]
    grid_size = cotangent.shape[2]
    mode_count = mode_scale.shape[1]
    bricks = lax.axis_size("brick")
    capacity = 3 * blocks // bricks
    slot_count = bricks * capacity
    local_rows = slab_planes * grid_size
    features = point_features.reshape(channels, blocks, 128)
    places = point_positions.reshape(3, blocks, 128)
    member = (owner_brick[:, None] == jnp.arange(bricks, dtype=jnp.int32)[None, :]).astype(
        jnp.int32
    )
    earlier = jnp.cumsum(member, axis=0) - member
    target = owner_brick * capacity + jnp.sum(earlier * member, axis=1)
    row_across = (owner_brick[:, None] * slab_planes + block_rows // grid_size).astype(jnp.float32)
    near_plane, near_line = kernels(
        places, row_across, (block_rows % grid_size).astype(jnp.float32), grid_size
    )
    contribution = contribute(features, near_plane, near_line)
    placing = (
        target[:, None] * pair_count + jnp.arange(pair_count, dtype=jnp.int32)[None, :]
    ).reshape(-1)
    part_send = (
        jnp.zeros((channels, slot_count * pair_count, grid_size), jnp.float32)
        .at[:, placing, :]
        .set(contribution.reshape(channels, -1, grid_size))
    )
    row_send = (
        jnp.full((1, slot_count * pair_count), local_rows, jnp.int32)
        .at[0, placing]
        .set(block_rows.reshape(-1))
    )
    got_parts, got_rows = (
        lax.all_to_all(
            part_send.astype(jnp.bfloat16), "brick", split_axis=1, concat_axis=1, tiled=True
        ).astype(part_send.dtype),
        lax.all_to_all(row_send, "brick", split_axis=1, concat_axis=1, tiled=True),
    )
    flat_rows = got_rows[0]
    summed = (
        jnp.zeros((channels, local_rows, grid_size), jnp.float32)
        .at[:, flat_rows, :]
        .add(got_parts, mode="drop")
    )
    encoded = summed.reshape(channels, slab_planes, grid_size, grid_size).astype(jnp.bfloat16)
    cosine_table, sine_table, line_table = spectral_tables(grid_size, mode_count)
    cell_share = 1.0 / (grid_size * grid_size * grid_size)
    shared_line = (line_table.astype(jnp.float32) * cell_share).astype(jnp.bfloat16)
    z_modes = jnp.einsum(
        "cxyz,zr->cxyr", encoded, line_table, preferred_element_type=jnp.float32
    ).astype(jnp.bfloat16)
    y_modes = fourier_section("cxyr,yk->cxkr", z_modes, cosine_table, sine_table, 1.0).astype(
        jnp.bfloat16
    )
    modes = fourier_section("cxkr,xj->cjkr", into_modes(y_modes), cosine_table, sine_table, 1.0)
    scaled = complex_times(mode_scale, modes, False)
    mixed_modes = jnp.einsum(
        "dc,cjkr->djkr", channel_mix, scaled, precision=lax.Precision.HIGHEST
    ).astype(jnp.bfloat16)
    back_x = fourier_section("cjkr,xj->cxkr", mixed_modes, cosine_table, sine_table, -1.0).astype(
        jnp.bfloat16
    )
    back_y = fourier_section(
        "cxkr,yk->cxyr", into_slabs(back_x), cosine_table, sine_table, -1.0
    ).astype(jnp.bfloat16)
    spectral = jnp.einsum("cxyr,zr->cxyz", back_y, shared_line, preferred_element_type=jnp.float32)
    pre_act = spectral + jnp.einsum(
        "dc,cxyz->dxyz", skip_weight, encoded, preferred_element_type=jnp.float32
    )
    latent_grid = jax.nn.gelu(pre_act).astype(jnp.bfloat16)
    _, gelu_back = jax.vjp(jax.nn.gelu, pre_act)
    grad_pre = gelu_back(cotangent.astype(jnp.float32))[0].astype(jnp.bfloat16)
    grad_zmodes = jnp.einsum(
        "cxyz,zr->cxyr", grad_pre, shared_line, preferred_element_type=jnp.float32
    ).astype(jnp.bfloat16)
    grad_ymodes = fourier_section(
        "cxyr,yk->cxkr", grad_zmodes, cosine_table, sine_table, 1.0
    ).astype(jnp.bfloat16)
    grad_modes = fourier_section(
        "cxkr,xj->cjkr", into_modes(grad_ymodes), cosine_table, sine_table, 1.0
    )
    local_mix = jnp.einsum("djkr,cjkr->dc", grad_modes, scaled, precision=lax.Precision.HIGHEST)
    mix_grads = lax.psum(local_mix, "brick") / grid_size
    grad_scaled = jnp.einsum(
        "dc,djkr->cjkr", channel_mix, grad_modes, precision=lax.Precision.HIGHEST
    )
    grad_spec = complex_times(mode_scale, grad_scaled, True).astype(jnp.bfloat16)
    grad_back_x = fourier_section(
        "cjkr,xj->cxkr", grad_spec, cosine_table, sine_table, -1.0
    ).astype(jnp.bfloat16)
    grad_back_y = fourier_section(
        "cxkr,yk->cxyr", into_slabs(grad_back_x), cosine_table, sine_table, -1.0
    ).astype(jnp.bfloat16)
    grad_encoded = jnp.einsum(
        "cxyr,zr->cxyz", grad_back_y, line_table, preferred_element_type=jnp.float32
    )
    grad_encoded = grad_encoded + jnp.einsum(
        "dc,dxyz->cxyz", skip_weight, grad_pre, preferred_element_type=jnp.float32
    )
    flat_grad = grad_encoded.astype(jnp.bfloat16).reshape(channels, local_rows, grid_size)
    safe_rows = jnp.minimum(flat_rows, local_rows - 1)
    sent_rows = jnp.take(flat_grad, safe_rows, axis=1)
    returned = lax.all_to_all(sent_rows, "brick", split_axis=1, concat_axis=1, tiled=True)
    rows_grad = jnp.take(returned, placing, axis=1).reshape(channels, blocks, pair_count, grid_size)
    point_grads = (
        pull_back(rows_grad, near_plane, near_line).astype(jnp.bfloat16).reshape(channels, points)
    )
    return (latent_grid, point_grads, mix_grads)


def solution(mesh):
    in_specs = (
        P(None, ("groups", "brick")),
        P(None, ("groups", "brick")),
        P(("groups", "brick")),
        P(("groups", "brick"), None),
        P(None, None, "brick", None),
        P(),
        P(),
        P(None, ("groups", "brick"), None, None),
    )
    out_specs = (
        P(None, ("groups", "brick"), None, None),
        P(None, ("groups", "brick")),
        P("groups", None),
    )
    return jax.shard_map(shards, mesh=mesh, in_specs=in_specs, out_specs=out_specs, check_vma=False)
```

profile of v0, /device:TPU:1, one launch (start us, length us, event | category | flops | bytes accessed | tf_op | source)
XLA Modules:
  0.0 716.8 jit_solution(9799384026748469861)
XLA Ops:
  6.4 7.3 %all-to-all-start = ((s32[1,16,24]{2,0,1:T(1,128)}), s32[1,16,24]{2,0,1:T(1,128)S(1)}, u32[]{:S(2)}, u32[]{:S(2)}) async-start(s32[1,16,24]{2,0,1:T(1,128)} %all_to_all.64), calls=%async_computation | async-start | bytes 16384 | tf_op jit(solution)/shard_map/all_to_all | solution.py:136
  17.0 3.5 broadcast_in_dim.22
  20.5 15.7 %scatter_fusion = f32[32,384,128]{2,0,1:T(8,128)} fusion(f32[32,384,128]{2,0,1:T(8,128)} %broadcast_in_dim.22, s32[128]{0:T(128)S(1)} %fusion.132, f32[128,32,128]{2,1,0:T(8,128)S(1)} %bitcast.301), kind=kCustom, calls=%fused_computation.3 | custom fusion | bytes 6291968 | tf_op jit(solution)/shard_map/scatter | solution.py:125
  36.2 5.2 convert_element_type.203
  41.4 6.0 all-to-all-start.1
  50.0 57.2 %all-to-all-done.1 = bf16[32,384,128]{2,0,1:T(8,128)(2,1)S(1)} async-done(((bf16[32,384,128]{2,0,1:T(8,128)(2,1)}), bf16[32,384,128]{2,0,1:T(8,128)(2,1)S(1)}, u32[]{:S(2)}, u32[]{:S(2)}) %all-to-all-start.1) | async-done | bytes 3145760 | tf_op jit(solution)/shard_map/all_to_all | solution.py:133
  107.2 3.6 convert_bitcast_fusion
  110.8 7.9 %broadcast_in_dim.20 = f32[32,1024,128]{2,0,1:T(8,128)} broadcast(f32[]{:T(128)} %constant.65.clone.1), dimensions={} | broadcast | bytes 16777220 | tf_op jit(solution)/shard_map/broadcast_in_dim | solution.py:140
  118.7 47.9 %scatter_fusion.1 = f32[32,1024,128]{2,0,1:T(8,128)} fusion(f32[32,1024,128]{2,0,1:T(8,128)} %broadcast_in_dim.20, s32[384]{0:T(512)S(1)} %get-tuple-element.6, f32[384,32,128]{2,1,0:T(8,128)} %convert_bitcast_fusion), kind=kCustom, calls=%fused_computation.4 | custom fusion | flops 1572864 | bytes 18875904 | tf_op jit(solution)/shard_map/scatter-add | solution.py:142
  166.6 7.1 convert_element_type.205
  173.8 9.5 %fusion.25 = bf16[32,8,128,64]{2,3,1,0:T(8,128)(2,1)S(1)} fusion(bf16[128,64,1,1]{0,1,3,2:T(8,128)(2,1)S(1)} %bitcast.303, bf16[32,8,128,128]{3,0,2,1:T(8,128)(2,1)S(1)} %bitcast.259), kind=kOutput, calls=%fused_computation.47 | convolution fusion | flops 538968064 | bytes 12599296 | tf_op jit(solution)/shard_map/cxyz,zr->cxyr/dot_general | solution.py:148
  185.3 6.1 convolution_bitcast_fusion.1
  191.4 7.3 %copy.224 = f32[32,8,32,64]{2,1,3,0:T(8,128)} copy(f32[32,8,32,64]{3,2,1,0:T(8,128)} %convolution_bitcast_fusion.1) | data formatting | bytes 4194304 | tf_op jit(solution)/shard_map/cxyr,yk->cxkr/transpose | solution.py:32
  198.7 4.1 fusion.211
  202.7 4.1 pad_maximum_fusion
  206.9 6.8 copy.225
  213.7 7.6 %fusion.20 = bf16[32,8,32,64]{3,2,1,0:T(8,128)(2,1)S(1)} fusion(f32[32,8,32,64]{3,2,1,0:T(8,128)} %copy.225, bf16[32,8,128,64]{2,3,1,0:T(8,128)(2,1)} %copy-done.3, s32[32]{0:T(128)S(1)} %compare_select_fusion.5), kind=kOutput, calls=%fused_computation.43 | convolution fusion | flops 135327744 | bytes 7340160 | tf_op jit(solution)/shard_map/cxyr,yk->cxkr/dot_general | solution.py:31
  224.4 18.2 %all-to-all-start.2 = ((bf16[16,2,16384]{2,1,0:T(2,128)(2,1)}), bf16[16,2,16384]{2,1,0:T(2,128)(2,1)S(1)}, u32[]{:S(2)}, u32[]{:S(2)}) async-start(bf16[16,2,16384]{2,1,0:T(2,128)(2,1)} %reshape.401), calls=%async_computation.2 | async-start | bytes 2097152 | tf_op jit(solution)/shard_map/all_to_all | solution.py:80
  244.8 20.9 %all-to-all-done.2 = bf16[16,2,16384]{2,1,0:T(2,128)(2,1)S(1)} async-done(((bf16[16,2,16384]{2,1,0:T(2,128)(2,1)}), bf16[16,2,16384]{2,1,0:T(2,128)(2,1)S(1)}, u32[]{:S(2)}, u32[]{:S(2)}) %all-to-all-start.2) | async-done | bytes 1048608 | tf_op jit(solution)/shard_map/all_to_all | solution.py:80
  270.2 2.8 copy.230
  276.4 3.2 copy.231
  279.6 3.1 fusion.46
  282.7 4.1 copy.232
  290.4 2.9 copy.233
  295.0 2.5 slice_multiply_fusion.6
  300.3 4.3 copy.236
  304.6 5.8 reshape.403
  310.4 6.7 all-to-all-start.3
  317.0 11.5 %fusion.100 = f32[8,128,128,32]{2,3,1,0:T(8,128)} fusion(bf16[32,8,128,128]{3,0,2,1:T(8,128)(2,1)} %bitcast.260, bf16[32,32]{1,0:T(8,128)(2,1)S(1)} %copy-done.10), kind=kOutput, calls=%fused_computation.151 | convolution fusion | flops 268435456 | bytes 25167872 | tf_op jit(solution)/shard_map/dc,cxyz->dxyz/dot_general | solution.py:166
  328.5 11.7 %all-to-all-done.3 = bf16[16,2,16384]{2,1,0:T(2,128)(2,1)S(1)} async-done(((bf16[16,2,16384]{2,1,0:T(2,128)(2,1)}), bf16[16,2,16384]{2,1,0:T(2,128)(2,1)S(1)}, u32[]{:S(2)}, u32[]{:S(2)}) %all-to-all-start.3) | async-done | bytes 1048608 | tf_op jit(solution)/shard_map/all_to_all | solution.py:84
  342.5 4.0 copy.330
  350.5 6.6 slice_multiply_fusion.2
  357.1 9.2 %pad_maximum_fusion.1 = f32[32,8,128,32,2]{2,4,3,1,0:T(2,128)} fusion(f32[32,8,128,32,1]{2,4,3,1,0:T(1,128)S(1)} %get-tuple-element.14, f32[32,8,128,32,1]{2,4,3,1,0:T(1,128)S(1)} %get-tuple-element.13), kind=kLoop, calls=%fused_computation.24 | loop fusion | flops 2097152 | bytes 16777216 | tf_op jit(solution)/shard_map/stack | solution.py:26
  366.3 24.6 %fusion.2 = (bf16[32,8,128,128]{3,2,1,0:T(8,128)(2,1)}, bf16[32,8,128,128]{3,2,1,0:T(8,128)(2,1)}) fusion(bf16[32,8,128,128]{3,2,1,0:T(8,128)(2,1)} %param.15, f32[8,128,128,32]{2,3,1,0:T(8,128)} %fusion.100, bf16[128,64]{0,1:T(8,128)(2,1)S(1)} %bitcast.304, f32[32,8,128,64]{2,3,1,0:T(8,128)} %bitcast.282, bf16[32,8,32,64]{3,2,1,0:T(8,128)(2,1)} %bitcast.299, ...), kind=kOutput, calls=%fused_computation.11 | convolution fusion | flops 776032256 | bytes 51396736 | tf_op jit(solution)/shard_map/cxyr,zr->cxyz/dot_general | solution.py:165
  390.9 6.4 convolution_convert_fusion
  399.3 6.1 convolution_bitcast_fusion
  405.4 6.9 copy.241
  412.3 4.0 fusion.210
  416.4 4.1 pad_maximum_fusion.2
  420.5 6.8 copy.242
  427.3 7.6 %fusion.19 = bf16[32,8,32,64]{3,2,1,0:T(8,128)(2,1)S(1)} fusion(f32[32,8,32,64]{3,2,1,0:T(8,128)} %copy.242, bf16[32,8,128,64]{2,3,1,0:T(8,128)(2,1)} %copy-done.2, s32[32]{0:T(128)S(1)} %compare_select_fusion.5), kind=kOutput, calls=%fused_computation.41 | convolution fusion | flops 135327744 | bytes 7340160 | tf_op jit(solution)/shard_map/cxyr,yk->cxkr/dot_general | solution.py:31
  437.2 3.9 reshape.405
  441.1 32.0 %all_to_all.91 = bf16[16,2,16384]{2,1,0:T(2,128)(2,1)} all-to-all(bf16[16,2,16384]{2,1,0:T(2,128)(2,1)S(1)} %reshape.405), channel_id=1, replica_groups=mesh['groups'=2,'brick'=16] {'brick'}, dimensions={0} | all-to-all | bytes 2097152 | tf_op jit(solution)/shard_map/all_to_all | solution.py:80
  473.0 4.7 reshape.406
  479.9 2.8 copy.247
  486.0 3.2 copy.248
  494.1 3.0 copy.251
  501.2 2.5 slice_multiply_fusion.4
  506.5 2.9 copy.254
  511.7 4.6 all-to-all-start.5
  516.4 14.2 %fusion.13 = f32[8,128,128,32]{2,3,1,0:T(8,128)} fusion(bf16[32,8,128,128]{3,2,1,0:T(8,128)(2,1)} %get-tuple-element.7, bf16[32,32]{1,0:T(8,128)(2,1)S(1)} %copy-done.10), kind=kOutput, calls=%fused_computation.31 | convolution fusion | flops 268435456 | bytes 25167872 | tf_op jit(solution)/shard_map/dc,dxyz->cxyz/dot_general | solution.py:196
  530.6 8.8 %all-to-all-done.5 = bf16[16,2,16384]{2,1,0:T(2,128)(2,1)S(1)} async-done(((bf16[16,2,16384]{2,1,0:T(2,128)(2,1)}), bf16[16,2,16384]{2,1,0:T(2,128)(2,1)S(1)}, u32[]{:S(2)}, u32[]{:S(2)}) %all-to-all-start.5) | async-done | bytes 1048608 | tf_op jit(solution)/shard_map/all_to_all | solution.py:84
  541.2 2.4 copy.329
  547.6 6.6 slice_multiply_fusion
  554.2 9.2 %pad_maximum_fusion.3 = f32[32,8,128,32,2]{2,4,3,1,0:T(2,128)} fusion(f32[32,8,128,32,1]{2,4,3,1,0:T(1,128)S(1)} %get-tuple-element.10, f32[32,8,128,32,1]{2,4,3,1,0:T(1,128)S(1)} %get-tuple-element.9), kind=kLoop, calls=%fused_computation.26 | loop fusion | flops 2097152 | bytes 16777216 | tf_op jit(solution)/shard_map/stack | solution.py:26
  563.4 15.3 %fusion.10 = bf16[32,8,128,128]{3,2,1,0:T(8,128)(2,1)} fusion(f32[8,128,128,32]{2,3,1,0:T(8,128)} %fusion.13, bf16[128,64,1,1]{0,1,3,2:T(8,128)(2,1)S(1)} %bitcast.306, f32[32,8,128,64]{2,3,1,0:T(8,128)} %bitcast.261, bf16[32,8,32,64]{3,2,1,0:T(8,128)(2,1)S(1)} %bitcast.278, s32[32]{0:T(128)S(1)} %compare_select_fusion.5), kind=kOutput, calls=%fused_computation.20 | convolution fusion | flops 683732992 | bytes 34619520 | tf_op jit(solution)/shard_map/cxyr,zr->cxyz/dot_general | solution.py:193
  578.6 12.0 %copy.260 = bf16[32,1024,128]{2,0,1:T(8,128)(2,1)} copy(bf16[32,1024,128]{2,1,0:T(8,128)(2,1)} %bitcast.262) | data formatting | bytes 16777216 | tf_op jit(solution)/shard_map/reshape | solution.py:199
  590.6 4.6 gather_fusion
  595.3 2.5 select_bitcast_fusion
  597.8 6.9 all-to-all-start.6
  604.9 2.8 copy.262
  607.7 3.5 convolution_bitcast_fusion.3
  611.2 100.5 %psum.7 = f32[32,32]{1,0:T(8,128)S(1)} all-reduce(f32[32,32]{1,0:T(8,128)S(1)} %convolution_bitcast_fusion.3), channel_id=1, replica_groups=mesh['groups'=2,'brick'=16] {'brick'}, use_global_device_ids=true, to_apply=%region_6.7 | all-reduce | flops 1024 | bytes 8192 | tf_op jit(solution)/shard_map/psum | solution.py:182
  712.4 2.6 gather_fusion.1
  (107 shorter events, 72.4 us)
Async XLA Ops:
  0.6 292.7 %copy-start = (f32[32,32]{1,0:T(8,128)S(1)}, f32[32,32]{1,0:T(8,128)}, u32[]{:S(2)}) copy-start(f32[32,32]{1,0:T(8,128)} %param.13) | copy-start | bytes 12292
  2.9 1.5 copy-start.17
  4.6 15.9 %copy-start.15 = (s32[128]{0:T(128)}, s32[128]{0:T(128)S(1)}, u32[]{:S(2)}) copy-start(s32[128]{0:T(128)S(1)} %fusion.132) | copy-start | bytes 1540
  6.4 35.0 %all-to-all-start = ((s32[1,16,24]{2,0,1:T(1,128)}), s32[1,16,24]{2,0,1:T(1,128)S(1)}, u32[]{:S(2)}, u32[]{:S(2)}) async-start(s32[1,16,24]{2,0,1:T(1,128)} %all_to_all.64), calls=%async_computation | async-start | bytes 16384 | tf_op jit(solution)/shard_map/all_to_all | solution.py:136
  14.9 5.6 copy-start.12
  16.1 0.9 copy-start.8
  41.4 65.7 %all-to-all-start.1 = ((bf16[32,384,128]{2,0,1:T(8,128)(2,1)}), bf16[32,384,128]{2,0,1:T(8,128)(2,1)S(1)}, u32[]{:S(2)}, u32[]{:S(2)}) async-start(bf16[32,384,128]{2,0,1:T(8,128)(2,1)} %convert_element_type.203), calls=%async_computation.1 | async-start | bytes 6291456 | tf_op jit(solution)/shard_map/all_to_all | solution.py:133
  173.8 9.5 %copy-start.1 = (bf16[32,1024,128]{2,0,1:T(8,128)(2,1)}, bf16[32,1024,128]{2,0,1:T(8,128)(2,1)S(1)}, u32[]{:S(2)}) copy-start(bf16[32,1024,128]{2,0,1:T(8,128)(2,1)S(1)} %convert_element_type.205) | copy-start | bytes 25165828
  183.3 2.0 copy-start.3
  224.4 41.3 %all-to-all-start.2 = ((bf16[16,2,16384]{2,1,0:T(2,128)(2,1)}), bf16[16,2,16384]{2,1,0:T(2,128)(2,1)S(1)}, u32[]{:S(2)}, u32[]{:S(2)}) async-start(bf16[16,2,16384]{2,1,0:T(2,128)(2,1)} %reshape.401), calls=%async_computation.2 | async-start | bytes 2097152 | tf_op jit(solution)/shard_map/all_to_all | solution.py:80
  300.3 16.7 %copy-start.10 = (bf16[32,32]{1,0:T(8,128)(2,1)S(1)}, bf16[32,32]{1,0:T(8,128)(2,1)}, u32[]{:S(2)}) copy-start(bf16[32,32]{1,0:T(8,128)(2,1)} %param.14) | copy-start | bytes 6148
  310.4 29.8 %all-to-all-start.3 = ((bf16[16,2,16384]{2,1,0:T(2,128)(2,1)}), bf16[16,2,16384]{2,1,0:T(2,128)(2,1)S(1)}, u32[]{:S(2)}, u32[]{:S(2)}) async-start(bf16[16,2,16384]{2,1,0:T(2,128)(2,1)} %reshape.403), calls=%async_computation.3 | async-start | bytes 2097152 | tf_op jit(solution)/shard_map/all_to_all | solution.py:84
  348.7 1.8 copy-start.7
  397.3 2.0 copy-start.2
  491.4 1.0 copy-start.5
  506.4 9.9 %copy-start.11 = (s32[16,24]{1,0:T(8,128)S(1)}, s32[16,24]{1,0:T(8,128)}, u32[]{:S(2)}) copy-start(s32[16,24]{1,0:T(8,128)} %get-tuple-element.3) | copy-start | bytes 4612
  506.4 9.9 %copy-start.14 = (s32[384]{0:T(512)S(1)}, s32[384]{0:T(512)}, u32[]{:S(2)}) copy-start(s32[384]{0:T(512)} %get-tuple-element.5) | copy-start | bytes 4612
  511.7 27.8 %all-to-all-start.5 = ((bf16[16,2,16384]{2,1,0:T(2,128)(2,1)}), bf16[16,2,16384]{2,1,0:T(2,128)(2,1)S(1)}, u32[]{:S(2)}, u32[]{:S(2)}) async-start(bf16[16,2,16384]{2,1,0:T(2,128)(2,1)} %reshape.407), calls=%async_computation.5 | async-start | bytes 2097152 | tf_op jit(solution)/shard_map/all_to_all | solution.py:84
  597.8 7.0 copy-start.18
  597.8 7.1 copy-start.16
  597.8 7.1 copy-start.6
  597.8 10.0 %copy-start.4 = (f32[32,32,2,32,2]{1,0,4,3,2:T(8,128)S(1)}, f32[32,32,2,32,2]{1,0,4,3,2:T(8,128)}, u32[]{:S(2)}) copy-start(f32[32,32,2,32,2]{1,0,4,3,2:T(8,128)} %pad_maximum_fusion.5) | copy-start | bytes 1572868
  597.8 114.6 %all-to-all-start.6 = ((bf16[32,384,128]{2,0,1:T(8,128)(2,1)}), bf16[32,384,128]{2,0,1:T(8,128)(2,1)}, u32[]{:S(2)}, u32[]{:S(2)}) async-start(bf16[32,384,128]{2,0,1:T(8,128)(2,1)} %select_bitcast_fusion), calls=%async_computation.6 | async-start | bytes 6291456 | tf_op jit(solution)/shard_map/all_to_all | solution.py:202
  604.9 110.2 %copy-start.9 = (f32[32,4,128]{2,1,0:T(4,128)S(1)}, f32[32,4,128]{2,1,0:T(4,128)}, u32[]{:S(2)}) copy-start(f32[32,4,128]{2,1,0:T(4,128)} %copy-done.8) | copy-start | bytes 196612
  604.9 110.2 %copy-start.13 = (f32[1,4096]{1,0:T(1,128)S(1)}, f32[1,4096]{1,0:T(1,128)}, u32[]{:S(2)}) copy-start(f32[1,4096]{1,0:T(1,128)} %copy-done.12) | copy-start | bytes 49156
where the time goes:
time: 727 us; the launch traced here: 717 us
  local copies, waits for them, and re-layouts  159 us (22%)
  other arithmetic  143 us (20%)
  matrix products  132 us (18%)
  blocking collectives  132 us (18%)
  waiting for transfers between devices  98.6 us (14%)
  starting transfers between devices  49.8 us (7%)
    psum x1, blocking collectives, shards(): mix_grads = lax.psum(local_mix, 'brick') / grid_size  101 us
    all_to_all x1, waiting for transfers between devices, shards(): lax.all_to_all(part_send.astype(jnp.bfloat16), 'brick', split_axis=1, con...  57.2 us
    scatter-add x1, other arithmetic, shards(): summed = jnp.zeros((channels, local_rows, grid_size), jnp.float32).at[:,...  47.9 us
    another operation x8, other arithmetic, rotate(): jnp.stack([direction * paired[..., 1], -direction * paired[..., 0]], axis...  33.9 us
    unnamed x48, local copies, waits for them, and re-layouts  33.2 us
    all_to_all x1, blocking collectives, into_modes(): lax.all_to_all(values, 'brick', split_axis=2, concat_axis=1, tiled=True)  32 us
    dot_general x1, matrix products, shards(): jnp.einsum('cxyr,zr->cxyz', back_y, shared_line, preferred_element_type=j...  24.6 us
    dot_general x6, matrix products, fourier_section(): jnp.einsum(pattern, values, cosine_table, preferred_element_type=jnp.floa...  21.8 us
  transfers between devices with their start and end apart: 6, of which 4 were waited for; matrix products, arithmetic and copies ran while one was open for 9% of the time, Pallas kernels for 0%

commit v1 on v0

v1 whole, which is shorter than its diff:
```python
import math

import jax
import jax.numpy as jnp
import numpy as np
from jax import lax
from jax.experimental import pallas as pl
from jax.experimental.pallas import tpu as pltpu
from jax.sharding import PartitionSpec as P

F32 = jnp.float32
BF16 = jnp.bfloat16
VMEM_BYTES = 56 * 1024 * 1024


def rounded(values):
    return np.asarray(values, np.float32).astype(jnp.bfloat16).astype(np.float32)


def tables(grid, modes, bricks, planes, own_modes):
    place = np.arange(grid)
    numbers = np.arange(modes)
    signed = np.where(numbers < modes // 2, numbers, numbers - modes)
    turns = (place[:, None] * signed[None, :] % grid) * (2.0 * math.pi / grid)
    cosine, sine = rounded(np.cos(turns)), rounded(np.sin(turns))
    line_turns = (place[:, None] * numbers[None, :] % grid) * (2.0 * math.pi / grid)
    line = np.stack([np.cos(line_turns), -np.sin(line_turns)], axis=-1)
    line = rounded(line.reshape(grid, 2 * modes))
    turn = np.zeros((2 * modes, 2 * modes), np.float32)
    turn[2 * numbers + 1, 2 * numbers] = 1.0
    turn[2 * numbers, 2 * numbers + 1] = -1.0
    two = np.eye(2, dtype=np.float32)
    z_in = np.concatenate([np.kron(two, line), np.kron(two, line @ turn)], axis=1)
    y_in = np.concatenate([cosine.T, sine.T], axis=1)
    z_out = np.concatenate([np.kron(two, line.T), np.kron(two, turn @ line.T)], axis=1)
    y_out = np.concatenate([cosine, -sine], axis=1)
    x_in = np.zeros((2, own_modes, modes, bricks, own_modes, planes), np.float32)
    x_out = np.zeros((bricks, own_modes, planes, 2, own_modes, modes), np.float32)
    by_brick_cos = cosine.reshape(bricks, planes, modes)
    by_brick_sin = sine.reshape(bricks, planes, modes)
    for k in range(own_modes):
        x_in[0, k, :, :, k, :] = by_brick_cos.transpose(2, 0, 1)
        x_in[1, k, :, :, k, :] = by_brick_sin.transpose(2, 0, 1)
        x_out[:, k, :, 0, k, :] = by_brick_cos
        x_out[:, k, :, 1, k, :] = -by_brick_sin
    rows = bricks * own_modes * planes
    x_in = x_in.reshape(2 * own_modes * modes, rows)
    x_out = x_out.reshape(rows, 2 * own_modes * modes)
    return z_in, y_in, z_out, y_out, x_in, x_out


def dot(left, right):
    return jnp.dot(left, right, preferred_element_type=F32)


def is_even(shape):
    return lax.broadcasted_iota(jnp.int32, shape, 1) % 2 == 0


def rotate(values, even):
    return jnp.where(even, pltpu.roll(values, 127, 1), -pltpu.roll(values, 1, 1))


def near_rows(block):
    dx = block[32:33] + block[33:34]
    dy = block[34:35] + block[35:36]
    return [jnp.exp(-0.5 * (dx * dx + (dy + float(j)) * (dy + float(j)))) for j in range(4)]


def near_line_of(block, grid):
    depth = lax.broadcasted_iota(jnp.int32, (grid, 128), 0).astype(F32)
    away = (depth - block[36:37]) - (block[37:38] + block[38:39])
    return jnp.exp(-0.5 * away * away).astype(BF16)


def forward_lines(first, second, z_in, y_in):
    pair = jnp.concatenate([first.astype(BF16), second.astype(BF16)], axis=1)
    both = dot(pair, z_in).astype(BF16)
    return dot(y_in, jnp.concatenate([both[:, :128], both[:, 128:]], axis=0))


def inverse_lines(values, z_out, y_out):
    both = dot(values.astype(BF16), z_out).astype(BF16)
    return dot(y_out, jnp.concatenate([both[:, :256], both[:, 256:]], axis=0))


def encode_kernel(capacity, planes, grid, base, got, z_in, y_in, encoded, y_modes, total, held):
    x = pl.program_id(0)
    channels = got.shape[1] - 8
    line_rows = grid * channels
    modes = y_in.shape[0]
    exchange_rows = modes * planes

    @pl.when(x == 0)
    def _():
        @pl.loop(0, total.shape[0] // 512)
        def _(i):
            total[pl.ds(pl.multiple_of(i * 512, 512), 512), :] = jnp.zeros((512, 128), F32)

        @pl.loop(0, got.shape[0] // capacity)
        def _(i):
            sums = []
            for s in range(capacity):
                block = got[i * capacity + s].astype(F32)
                weighted = jnp.concatenate(
                    [(block[:channels] * near).astype(BF16) for near in near_rows(block)], axis=0
                )
                sums.append(
                    lax.dot_general(
                        weighted,
                        near_line_of(block, grid),
                        (((1,), (1,)), ((), ())),
                        preferred_element_type=F32,
                    )
                )
            for s in range(capacity):
                start = pl.multiple_of(base[i * capacity + s] * channels, channels)
                total[pl.ds(start, 4 * channels), :] += sums[s]

    start = pl.multiple_of(x * line_rows, line_rows)
    encoded[...] = total[pl.ds(start, line_rows), :].astype(BF16)

    for p in range(channels // 2):
        out = forward_lines(
            total[pl.ds(start + 2 * p, grid, stride=channels), :],
            total[pl.ds(start + 2 * p + 1, grid, stride=channels), :],
            z_in[...],
            y_in[...],
        )
        held[pl.ds(p * exchange_rows + x, modes, stride=planes), :] = out

    @pl.when(x == planes - 1)
    def _():
        for p in range(channels // 2):
            y_modes[:, p * 128 : (p + 1) * 128] = held[
                p * exchange_rows : (p + 1) * exchange_rows, :
            ].astype(BF16)


def x_forward(got, x_in, even, rows):
    both = dot(x_in[...], got[...])
    parts = []
    for p in range(got.shape[1] // 128):
        span = slice(p * 128, (p + 1) * 128)
        parts.append(both[:rows, span] + rotate(both[rows:, span], even))
    return parts


def scale_parts(scale, even):
    real = jnp.where(even, scale, pltpu.roll(scale, 1, 1))
    imag = jnp.where(even, pltpu.roll(scale, 127, 1), scale)
    return real, imag


def mix_pairs(d, weights, straight, swapped, pairs):
    total = weights[d, 0:1, :] * straight[0] + weights[d, 1:2, :] * swapped[0]
    for p in range(1, pairs):
        total += weights[d, 2 * p : 2 * p + 1, :] * straight[p]
        total += weights[d, 2 * p + 1 : 2 * p + 2, :] * swapped[p]
    return total


def middle_kernel(got, x_in, x_out, scale, weights, scaled, back, straight, swapped):
    rows = scale.shape[0]
    pairs = got.shape[1] // 128
    even = is_even((rows, 128))
    for p, modes in enumerate(x_forward(got, x_in, even, rows)):
        span = slice(p * 128, (p + 1) * 128)
        real, imag = scale_parts(scale[:, span], even)
        value = modes * real - rotate(modes, even) * imag
        scaled[:, span] = value
        straight[p] = value
        swapped[p] = pltpu.roll(value, 64, 1)
    for d in range(pairs):
        mixed = mix_pairs(d, weights, straight, swapped, pairs)
        stacked = jnp.concatenate([mixed, rotate(mixed, even)], axis=0).astype(BF16)
        back[:, d * 128 : (d + 1) * 128] = dot(x_out[...], stacked).astype(BF16)


def middle_grad_kernel(
    got, x_in, x_out, scale, weights, scaled, back, products, straight, swapped
):
    rows = scale.shape[0]
    pairs = got.shape[1] // 128
    even = is_even((rows, 128))
    for p, grad in enumerate(x_forward(got, x_in, even, rows)):
        straight[p] = grad
        swapped[p] = pltpu.roll(grad, 64, 1)
    for c in range(pairs):
        span = slice(c * 128, (c + 1) * 128)
        mixed = mix_pairs(c, weights, straight, swapped, pairs)
        real, imag = scale_parts(scale[:, span], even)
        value = mixed * real + rotate(mixed, even) * imag
        stacked = jnp.concatenate([value, rotate(value, even)], axis=0).astype(BF16)
        back[:, span] = dot(x_out[...], stacked).astype(BF16)
    for c in range(pairs):
        value = scaled[:, c * 128 : (c + 1) * 128]
        for d in range(pairs):
            at = (c * pairs + d) * 2
            products[at : at + 1, :] = jnp.sum(value * straight[d], axis=0, keepdims=True)
            products[at + 1 : at + 2, :] = jnp.sum(value * swapped[d], axis=0, keepdims=True)


def spread(got, held):
    rows = got.shape[0]
    for p in range(got.shape[1] // 128):
        held[p * rows : (p + 1) * rows, :] = got[:, p * 128 : (p + 1) * 128].astype(F32)


def layer_kernel(
    planes,
    got,
    encoded,
    cotangent,
    skip,
    z_out,
    y_out,
    z_in,
    y_in,
    latent,
    grad_rows,
    y_modes,
    held,
    skipped,
    grads,
    held_out,
):
    x = pl.program_id(0)
    channels, grid = cotangent.shape[0], cotangent.shape[2]
    modes = y_in.shape[0]
    exchange_rows = modes * planes

    @pl.when(x == 0)
    def _():
        spread(got, held)

    for g in range(grid * channels // 256):
        skipped[g * 256 : (g + 1) * 256, :] = dot(skip[...], encoded[g * 256 : (g + 1) * 256, :])

    root = math.sqrt(2.0 / math.pi)

    @pl.loop(0, channels // 2)
    def _(p):
        values = held[pl.ds(p * exchange_rows + x, modes, stride=planes), :]
        spectral = inverse_lines(values, z_out[...], y_out[...])
        halves = []
        for h in range(2):
            d = 2 * p + h
            pre = spectral[:, h * 128 : (h + 1) * 128] + skipped[pl.ds(d, grid, stride=channels), :]
            square = pre * pre
            turned = jnp.tanh(pre * (root + (root * 0.044715) * square))
            gate = 0.5 + 0.5 * turned
            latent[d, 0] = (pre * gate).astype(BF16)
            slope = gate + (0.5 * pre) * (1.0 - turned * turned) * (
                root + (root * 3.0 * 0.044715) * square
            )
            grad = cotangent[d, 0].astype(F32) * slope
            grads[pl.ds(d, grid, stride=channels), :] = grad
            halves.append(grad)
        held_out[pl.ds(p * exchange_rows + x, modes, stride=planes), :] = forward_lines(
            halves[0], halves[1], z_in[...], y_in[...]
        )

    grad_rows[...] = grads[...].astype(BF16)

    @pl.when(x == planes - 1)
    def _():
        for p in range(channels // 2):
            y_modes[:, p * 128 : (p + 1) * 128] = held_out[
                p * exchange_rows : (p + 1) * exchange_rows, :
            ].astype(BF16)


def pull_kernel(
    capacity,
    planes,
    grid,
    base,
    got,
    back,
    grad_rows,
    skip,
    z_out,
    y_out,
    point_grads,
    held,
    rows_held,
    total,
    arrived,
):
    channels = point_grads.shape[1]
    exchange_rows = back.shape[0]
    modes = exchange_rows // planes
    copy = pltpu.make_async_copy(grad_rows, rows_held, arrived)
    copy.start()
    spread(back, held)

    @pl.loop(0, planes)
    def _(x):
        for p in range(channels // 2):
            values = held[pl.ds(p * exchange_rows + x, modes, stride=planes), :]
            lines = inverse_lines(values, z_out[...], y_out[...])
            for h in range(2):
                start = x * (grid * channels) + 2 * p + h
                total[pl.ds(start, grid, stride=channels), :] = lines[:, h * 128 : (h + 1) * 128]

    copy.wait()

    @pl.loop(0, got.shape[0] // capacity)
    def _(i):
        for s in range(capacity):
            block = got[i * capacity + s].astype(F32)
            start = pl.multiple_of(base[i * capacity + s] * channels, channels)
            span = pl.ds(start, 4 * channels)
            rows = total[span, :] + dot(skip[...], rows_held[span, :])
            near = dot(rows.astype(BF16), near_line_of(block, grid))
            summed = jnp.zeros((channels, 128), F32)
            for j, weight in enumerate(near_rows(block)):
                summed += near[j * channels : (j + 1) * channels] * weight
            point_grads[i * capacity + s] = summed.astype(BF16)


def vmem():
    return pl.BlockSpec(memory_space=pltpu.VMEM)


def params(**more):
    return pltpu.CompilerParams(vmem_limit_bytes=VMEM_BYTES, **more)


def whole(shape):
    return pl.BlockSpec(shape, lambda x: (0,) * len(shape))


def pair_weights(mix):
    channels = mix.shape[0]
    pairs = channels // 2
    cut = mix.reshape(pairs, 2, pairs, 2)
    straight = jnp.stack([cut[:, 0, :, 0], cut[:, 1, :, 1]], axis=-1)
    swapped = jnp.stack([cut[:, 0, :, 1], cut[:, 1, :, 0]], axis=-1)
    both = jnp.stack([straight, swapped], axis=2).reshape(pairs, channels, 2)
    return jnp.repeat(both, 64, axis=-1)


def exchange(values):
    return lax.all_to_all(values, "brick", split_axis=0, concat_axis=0, tiled=True)


def shards(
    point_features,
    point_positions,
    owner_brick,
    block_rows,
    mode_scale,
    channel_mix,
    skip_weight,
    cotangent,
):
    channels, points = point_features.shape
    blocks = points // 128
    planes, grid = cotangent.shape[1], cotangent.shape[2]
    mode_count, own_modes = mode_scale.shape[1], mode_scale.shape[2]
    bricks = lax.axis_size("brick")
    capacity = 3 * blocks // bricks
    slots = bricks * capacity
    local_rows = planes * grid
    width = channels * 2 * mode_count
    exchange_rows = mode_count * planes
    line_rows = grid * channels
    pairs = channels // 2
    z_in, y_in, z_out, y_out, x_in, x_out = tables(grid, mode_count, bricks, planes, own_modes)
    share = 1.0 / (grid * grid * grid)

    member = (owner_brick[:, None] == jnp.arange(bricks, dtype=jnp.int32)[None, :]).astype(
        jnp.int32
    )
    earlier = jnp.cumsum(member, axis=0) - member
    target = owner_brick * capacity + jnp.sum(earlier * member, axis=1)
    chosen = (jnp.arange(slots, dtype=jnp.int32)[:, None] == target[None, :]).astype(BF16)
    first_row = jnp.min(block_rows, axis=1)
    plane, along = first_row // grid, first_row % grid
    places = point_positions.reshape(3, blocks, 128)
    dx = (owner_brick * planes + plane).astype(F32)[:, None] - places[0]
    dy = along.astype(F32)[:, None] - places[1]
    cell = jnp.round(places[2])
    dz = places[2] - cell

    def head(values):
        return lax.reduce_precision(values, 8, 7)

    lanes = jnp.arange(128, dtype=jnp.int32)[None, :]
    named = jnp.where(lanes < 64, plane[:, None], along[:, None]).astype(F32)
    extra = jnp.stack(
        [head(dx), dx - head(dx), head(dy), dy - head(dy), cell, head(dz), dz - head(dz), named],
        axis=1,
    ).astype(BF16)
    features = point_features.reshape(channels, blocks, 128).transpose(1, 0, 2)
    sent = jnp.concatenate([features, extra], axis=1)
    sent = jnp.einsum("sb,brp->srp", chosen, sent, preferred_element_type=F32).astype(BF16)
    got = exchange(sent)
    ids = got[:, channels + 7, :].astype(F32).astype(jnp.int32)
    base = jnp.clip(ids[:, 0] * grid + ids[:, 64], 0, local_rows - 4)

    table = lambda values: jnp.asarray(values, BF16)
    smem = pl.BlockSpec(memory_space=pltpu.SMEM)
    encoded, y_modes = pl.pallas_call(
        lambda *refs: encode_kernel(capacity, planes, grid, *refs),
        grid=(planes,),
        in_specs=[smem, whole(got.shape), whole(z_in.shape), whole(y_in.shape)],
        out_specs=[
            pl.BlockSpec((line_rows, 128), lambda x: (x, 0)),
            whole((exchange_rows, width)),
        ],
        out_shape=[
            jax.ShapeDtypeStruct((planes * line_rows, 128), BF16),
            jax.ShapeDtypeStruct((exchange_rows, width), BF16),
        ],
        scratch_shapes=[
            pltpu.VMEM((planes * line_rows, 128), F32),
            pltpu.VMEM((pairs * exchange_rows, 128), F32),
        ],
        compiler_params=params(),
        name="encode",
    )(base, got, table(z_in), table(y_in))

    scale = mode_scale.transpose(2, 1, 0, 3).reshape(own_modes * mode_count, width)
    held_modes = pltpu.VMEM((pairs, own_modes * mode_count, 128), F32)
    scaled, back = pl.pallas_call(
        middle_kernel,
        in_specs=[vmem()] * 5,
        out_specs=[vmem()] * 2,
        out_shape=[
            jax.ShapeDtypeStruct(scale.shape, F32),
            jax.ShapeDtypeStruct((exchange_rows, width), BF16),
        ],
        scratch_shapes=[held_modes, held_modes],
        compiler_params=params(),
        name="middle",
    )(exchange(y_modes), table(x_in), table(x_out), scale, pair_weights(channel_mix))

    eye8 = jnp.eye(256 // channels, dtype=BF16)
    eye4 = jnp.eye(4, dtype=BF16)
    planes_spec = pl.BlockSpec((channels, 1, grid, grid), lambda x: (0, x, 0, 0))
    rows_spec = pl.BlockSpec((line_rows, 128), lambda x: (x, 0))
    latent_grid, grad_rows, grad_y_modes = pl.pallas_call(
        lambda *refs: layer_kernel(planes, *refs),
        grid=(planes,),
        in_specs=[
            whole((exchange_rows, width)),
            rows_spec,
            planes_spec,
            whole((256, 256)),
            whole(z_out.shape),
            whole(y_out.shape),
            whole(z_in.shape),
            whole(y_in.shape),
        ],
        out_specs=[planes_spec, rows_spec, whole((exchange_rows, width))],
        out_shape=[
            jax.ShapeDtypeStruct(cotangent.shape, BF16),
            jax.ShapeDtypeStruct((planes * line_rows, 128), BF16),
            jax.ShapeDtypeStruct((exchange_rows, width), BF16),
        ],
        scratch_shapes=[
            pltpu.VMEM((pairs * exchange_rows, 128), F32),
            pltpu.VMEM((line_rows, 128), F32),
            pltpu.VMEM((line_rows, 128), F32),
            pltpu.VMEM((pairs * exchange_rows, 128), F32),
        ],
        compiler_params=params(),
        name="layer",
    )(
        exchange(back),
        encoded,
        cotangent,
        jnp.kron(eye8, skip_weight),
        table(z_out * share),
        table(y_out),
        table(z_in * share),
        table(y_in),
    )

    grad_back, products = pl.pallas_call(
        middle_grad_kernel,
        in_specs=[vmem()] * 6,
        out_specs=[vmem()] * 2,
        out_shape=[
            jax.ShapeDtypeStruct((exchange_rows, width), BF16),
            jax.ShapeDtypeStruct((2 * pairs * pairs, 128), F32),
        ],
        scratch_shapes=[held_modes, held_modes],
        compiler_params=params(),
        name="middle_grad",
    )(
        exchange(grad_y_modes),
        table(x_in),
        table(x_out),
        scale,
        pair_weights(channel_mix.T),
        scaled,
    )
    by_half = jnp.sum(products.reshape(pairs, pairs, 2, 2, 64), axis=-1)
    by_part = jnp.stack(
        [
            jnp.stack([by_half[:, :, 0, 0], by_half[:, :, 1, 0]], axis=-1),
            jnp.stack([by_half[:, :, 1, 1], by_half[:, :, 0, 1]], axis=-1),
        ],
        axis=2,
    )
    local_mix = by_part.transpose(1, 3, 0, 2).reshape(channels, channels)
    mix_grads = lax.psum(local_mix, "brick") / grid

    pulled = pl.pallas_call(
        lambda *refs: pull_kernel(capacity, planes, grid, *refs),
        in_specs=[smem, vmem(), vmem(), pl.BlockSpec(memory_space=pl.ANY)] + [vmem()] * 3,
        out_specs=vmem(),
        out_shape=jax.ShapeDtypeStruct((slots, channels, 128), BF16),
        scratch_shapes=[
            pltpu.VMEM((pairs * exchange_rows, 128), F32),
            pltpu.VMEM((planes * line_rows, 128), BF16),
            pltpu.VMEM((planes * line_rows, 128), F32),
            pltpu.SemaphoreType.DMA,
        ],
        compiler_params=params(),
        name="pull",
    )(
        base,
        got,
        exchange(grad_back),
        grad_rows,
        jnp.kron(eye4, skip_weight.T),
        table(z_out),
        table(y_out),
    )
    returned = exchange(pulled)
    point_grads = jnp.einsum("sb,scp->cbp", chosen, returned, preferred_element_type=F32)
    return (latent_grid, point_grads.astype(BF16).reshape(channels, points), mix_grads)


def solution(mesh):
    in_specs = (
        P(None, ("groups", "brick")),
        P(None, ("groups", "brick")),
        P(("groups", "brick")),
        P(("groups", "brick"), None),
        P(None, None, "brick", None),
        P(),
        P(),
        P(None, ("groups", "brick"), None, None),
    )
    out_specs = (
        P(None, ("groups", "brick"), None, None),
        P(None, ("groups", "brick")),
        P("groups", None),
    )
    return jax.shard_map(shards, mesh=mesh, in_specs=in_specs, out_specs=out_specs, check_vma=False)
```

time: 727 us -> 395 us (0.54)
  Pallas kernels: 0 us -> 156 us
  local copies, waits for them, and re-layouts: 159 us -> 19.7 us
  other arithmetic: 143 us -> 6.06 us
  matrix products: 132 us -> 0.87 us
  blocking collectives: 132 us -> 90.8 us
  starting transfers between devices: 49.8 us -> 31.3 us
  waiting for transfers between devices: 98.6 us -> 83.5 us
    pallas_call x0 -> x5, Pallas kernels: none -> 156 us  [the longest x1 92.9 us: shards(): pl.pallas_call(lambda *refs: layer_kernel(planes, *refs), grid=(planes,),...]
    dot_general x25 -> x2, matrix products: 132 us -> 0.87 us  [the longest x1 0.53 us: shards(): jnp.einsum('sb,brp->srp', chosen, sent, preferred_element_type=F32)]
    scatter-add x1 -> x0, other arithmetic: 47.9 us -> none  [shards(): summed = jnp.zeros((channels, local_rows, grid_size), jnp.float32).at[:,...]
    psum x1, blocking collectives: 101 us -> 59.6 us  [shards(): mix_grads = lax.psum(local_mix, 'brick') / grid]
    another operation x11 -> x6, other arithmetic: 37.7 us -> 0.04 us  [the longest x4 0.03 us: pair_weights(): both = jnp.stack([straight, swapped], axis=2).reshape(pairs, channels, 2)]
    reshape x7 -> x9, local copies, waits for them, and re-layouts: 35.2 us -> 4.67 us  [the longest x2 2.03 us: pair_weights(): return jnp.repeat(both, 64, axis=-1)]
    unnamed x48 -> x21, local copies, waits for them, and re-layouts: 33.2 us -> 6.07 us
    transpose x4, local copies, waits for them, and re-layouts: 19.9 us -> 1.11 us  [the longest x1 0.61 us: shards(): mode_scale.transpose(2, 1, 0, 3).reshape(own_modes * mode_count, width)]
  transfers between devices with their start and end apart: 6 -> 5, of which waited for: 4 -> 4; matrix products, arithmetic and copies ran while one was open for 9% -> 4% of each run, Pallas kernels for 0% -> 0%
where the time goes in v1:
time: 395 us; the launch traced here: 389 us
  Pallas kernels  156 us (39%)
  blocking collectives  90.8 us (23%)
  waiting for transfers between devices  83.5 us (21%)
  starting transfers between devices  31.3 us (8%)
  local copies, waits for them, and re-layouts  19.7 us (5%)
  other arithmetic  6.06 us (2%)
    pallas_call x1, Pallas kernels, shards(): pl.pallas_call(lambda *refs: layer_kernel(planes, *refs), grid=(planes,),...  92.9 us
    all_to_all x5, waiting for transfers between devices, exchange(): lax.all_to_all(values, 'brick', split_axis=0, concat_axis=0, tiled=True)  83.5 us
    psum x1, blocking collectives, shards(): mix_grads = lax.psum(local_mix, 'brick') / grid  59.6 us
    all_to_all x5, starting transfers between devices, exchange(): lax.all_to_all(values, 'brick', split_axis=0, concat_axis=0, tiled=True)  31.3 us
    all_to_all x1, blocking collectives, exchange(): lax.all_to_all(values, 'brick', split_axis=0, concat_axis=0, tiled=True)  31.2 us
    pallas_call x1, Pallas kernels, shards(): pl.pallas_call(lambda *refs: encode_kernel(capacity, planes, grid, *refs)...  27.8 us
    pallas_call x1, Pallas kernels, shards(): pl.pallas_call(lambda *refs: pull_kernel(capacity, planes, grid, *refs),...  23.7 us
  transfers between devices with their start and end apart: 5, of which 4 were waited for; matrix products, arithmetic and copies ran while one was open for 4% of the time, Pallas kernels for 0%

profile of v1, /device:TPU:1, one launch (start us, length us, event | category | flops | bytes accessed | tf_op | source)
XLA Modules:
  0.0 389.4 jit_solution(1796279286911175792)
XLA Ops:
  0.7 0.8 fusion.7
  1.5 0.8 select_reduce_fusion
  2.4 1.0 fusion.17
  3.4 1.0 copy.113
  4.4 0.7 reduce_min.9
  5.1 0.7 add_convert_fusion
  5.8 0.1 constant_dynamic-update-slice_fusion.7
  5.9 0.1 constant_dynamic-update-slice_fusion.6
  5.9 0.1 constant_dynamic-update-slice_fusion.5
  6.0 0.1 constant_dynamic-update-slice_fusion.4
  6.1 0.1 constant_dynamic-update-slice_fusion
  6.2 0.5 fusion.10
  6.8 0.4 copy.119
  7.2 31.2 %all_to_all.54.refs_1_ = bf16[96,40,128]{2,1,0:T(8,128)(2,1)S(1)} all-to-all(bf16[96,40,128]{2,1,0:T(8,128)(2,1)S(1)} %copy.119), channel_id=1, replica_groups=mesh['groups'=2,'brick'=16] {'brick'}, dimensions={0} | all-to-all | bytes 1966080 | tf_op jit(solution)/shard_map/all_to_all | solution.py:346
  38.4 0.1 fusion.3
  38.4 0.8 fusion.2.refs_0_
  39.2 0.1 copy-done
  39.3 27.8 %encode.1 = (bf16[32768,128]{1,0:T(8,128)(2,1)}, bf16[256,2048]{1,0:T(8,128)(2,1)}) custom-call(s32[96]{0:T(128)} %fusion.2.refs_0_, bf16[96,40,128]{2,1,0:T(8,128)(2,1)} %copy-done, bf16[256,256]{1,0:T(8,128)(2,1)} %constant.65.clone.refs_2_, bf16[32,256]{1,0:T(8,128)(2,1)} %constant.66.clone.refs_3_.refs_7_), custom_call_target="tpu_custom_call" | custom-call | tf_op jit(solution)/shard_map/encode/pallas_call | solution.py:406
  67.2 4.4 %all-to-all-start.1 = ((bf16[16,16,2048]{2,1,0:T(8,128)(2,1)}), bf16[16,16,2048]{2,1,0:T(8,128)(2,1)S(1)}, u32[]{:S(2)}, u32[]{:S(2)}) async-start(bf16[16,16,2048]{2,1,0:T(8,128)(2,1)} %bitcast.69), calls=%async_computation.1 | async-start | bytes 2097152 | tf_op jit(solution)/shard_map/all_to_all | solution.py:346
  71.6 0.2 reshape.338
  71.8 0.3 slice_reduce_fusion.11
  72.1 0.1 copy.105
  72.2 0.3 copy.106
  72.5 0.6 broadcast_in_dim.50
  73.1 1.0 reshape.340.weights
  74.2 0.6 copy.104
  74.8 1.2 reshape.337.scale
  75.9 18.8 %all-to-all-done.1 = bf16[16,16,2048]{2,1,0:T(8,128)(2,1)S(1)} async-done(((bf16[16,16,2048]{2,1,0:T(8,128)(2,1)}), bf16[16,16,2048]{2,1,0:T(8,128)(2,1)S(1)}, u32[]{:S(2)}, u32[]{:S(2)}) %all-to-all-start.1) | async-done | bytes 1048608 | tf_op jit(solution)/shard_map/all_to_all | solution.py:346
  94.7 1.0 copy-done.3
  95.7 5.5 %middle.1 = (f32[64,2048]{1,0:T(8,128)}, bf16[256,2048]{1,0:T(8,128)(2,1)}) custom-call(bf16[256,2048]{1,0:T(8,128)(2,1)} %bitcast.65, bf16[128,256]{1,0:T(8,128)(2,1)} %constant.67.clone.x_in, bf16[256,128]{1,0:T(8,128)(2,1)} %constant.68.clone.x_out, f32[64,2048]{1,0:T(8,128)} %reshape.337.scale, f32[16,32,128]{2,1,0:T(8,128)} %reshape.340.weights), custom_call_target="tpu_custom_call" | custom-call | tf_op jit(solution)/shard_map/middle/pallas_call | solution.py:428
  101.3 6.7 %all-to-all-start.2 = ((bf16[16,16,2048]{2,1,0:T(8,128)(2,1)}), bf16[16,16,2048]{2,1,0:T(8,128)(2,1)S(1)}, u32[]{:S(2)}, u32[]{:S(2)}) async-start(bf16[16,16,2048]{2,1,0:T(8,128)(2,1)} %bitcast.71), calls=%async_computation.2 | async-start | bytes 2097152 | tf_op jit(solution)/shard_map/all_to_all | solution.py:346
  107.9 0.1 broadcast_multiply_fusion
  108.1 1.0 mul.80.refs_3_
  109.1 22.0 %all-to-all-done.2 = bf16[16,16,2048]{2,1,0:T(8,128)(2,1)S(1)} async-done(((bf16[16,16,2048]{2,1,0:T(8,128)(2,1)}), bf16[16,16,2048]{2,1,0:T(8,128)(2,1)S(1)}, u32[]{:S(2)}, u32[]{:S(2)}) %all-to-all-start.2) | async-done | bytes 1048608 | tf_op jit(solution)/shard_map/all_to_all | solution.py:346
  131.1 1.0 copy-done.4
  132.1 92.9 %layer.1 = (bf16[32,8,128,128]{3,2,1,0:T(8,128)(2,1)}, bf16[32768,128]{1,0:T(8,128)(2,1)}, bf16[256,2048]{1,0:T(8,128)(2,1)}) custom-call(bf16[256,2048]{1,0:T(8,128)(2,1)} %bitcast.66, bf16[32768,128]{1,0:T(8,128)(2,1)} %get-tuple-element.14.refs_1_, bf16[32,8,128,128]{3,2,1,0:T(8,128)(2,1)} %refs_2_.2, bf16[256,256]{1,0:T(8,128)(2,1)} %mul.80.refs_3_, ...), custom_call_target="tpu_custom_call" | custom-call | tf_op jit(solution)/shard_map/layer/pallas_call | solution.py:445
  225.0 6.7 %all-to-all-start.3 = ((bf16[16,16,2048]{2,1,0:T(8,128)(2,1)}), bf16[16,16,2048]{2,1,0:T(8,128)(2,1)S(1)}, u32[]{:S(2)}, u32[]{:S(2)}) async-start(bf16[16,16,2048]{2,1,0:T(8,128)(2,1)} %bitcast.68), calls=%async_computation.3 | async-start | bytes 2097152 | tf_op jit(solution)/shard_map/all_to_all | solution.py:346
  231.7 0.1 copy.107
  231.7 0.2 reshape.341
  231.9 0.3 slice_reduce_fusion.7
  232.2 0.1 copy.108
  232.3 0.3 copy.109
  232.7 0.6 broadcast_in_dim.51
  233.3 1.0 reshape.343.weights
  234.3 20.5 %all-to-all-done.3 = bf16[16,16,2048]{2,1,0:T(8,128)(2,1)S(1)} async-done(((bf16[16,16,2048]{2,1,0:T(8,128)(2,1)}), bf16[16,16,2048]{2,1,0:T(8,128)(2,1)S(1)}, u32[]{:S(2)}, u32[]{:S(2)}) %all-to-all-start.3) | async-done | bytes 1048608 | tf_op jit(solution)/shard_map/all_to_all | solution.py:346
  254.8 1.1 copy-done.2
  255.9 6.2 %middle_grad.1 = (bf16[256,2048]{1,0:T(8,128)(2,1)}, f32[512,128]{1,0:T(8,128)}) custom-call(bf16[256,2048]{1,0:T(8,128)(2,1)} %bitcast.64, bf16[128,256]{1,0:T(8,128)(2,1)} %constant.67.clone.x_in, bf16[256,128]{1,0:T(8,128)(2,1)} %constant.68.clone.x_out, f32[64,2048]{1,0:T(8,128)} %reshape.337.scale, f32[16,32,128]{2,1,0:T(8,128)} %reshape.343.weights, ...), custom_call_target="tpu_custom_call" | custom-call | tf_op jit(solution)/shard_map/middle_grad/pallas_call | solution.py:483
  262.1 6.8 %all-to-all-start.4 = ((bf16[16,16,2048]{2,1,0:T(8,128)(2,1)}), bf16[16,16,2048]{2,1,0:T(8,128)(2,1)S(1)}, u32[]{:S(2)}, u32[]{:S(2)}) async-start(bf16[16,16,2048]{2,1,0:T(8,128)(2,1)} %bitcast.70), calls=%async_computation.4 | async-start | bytes 2097152 | tf_op jit(solution)/shard_map/all_to_all | solution.py:346
  268.9 0.1 copy.110
  269.0 0.1 broadcast_multiply_fusion.1
  269.1 0.7 mul.84.refs_4_
  269.9 22.2 %all-to-all-done.4 = bf16[16,16,2048]{2,1,0:T(8,128)(2,1)S(1)} async-done(((bf16[16,16,2048]{2,1,0:T(8,128)(2,1)}), bf16[16,16,2048]{2,1,0:T(8,128)(2,1)S(1)}, u32[]{:S(2)}, u32[]{:S(2)}) %all-to-all-start.4) | async-done | bytes 1048608 | tf_op jit(solution)/shard_map/all_to_all | solution.py:346
  292.0 1.1 copy-done.1
  293.1 23.7 %pull.1 = bf16[96,32,128]{2,1,0:T(8,128)(2,1)} custom-call(s32[96]{0:T(128)} %fusion.2.refs_0_, bf16[96,40,128]{2,1,0:T(8,128)(2,1)} %copy-done, bf16[256,2048]{1,0:T(8,128)(2,1)} %bitcast.63, bf16[32768,128]{1,0:T(8,128)(2,1)} %get-tuple-element.19.refs_3_, bf16[128,128]{1,0:T(8,128)(2,1)} %mul.84.refs_4_, bf16[128,512]{1,0:T(8,128)(2,1)} %constant.72.clone.refs_5_, ...), custom_call_target="tpu_custom_call" | custom-call | tf_op jit(solution)/shard_map/pull/pallas_call | solution.py:513
  316.8 6.7 %all-to-all-start.5 = ((bf16[96,32,128]{2,1,0:T(8,128)(2,1)}), bf16[96,32,128]{2,1,0:T(8,128)(2,1)S(1)}, u32[]{:S(2)}, u32[]{:S(2)}) async-start(bf16[96,32,128]{2,1,0:T(8,128)(2,1)} %pull.1), calls=%async_computation.5 | async-start | bytes 1572864 | tf_op jit(solution)/shard_map/all_to_all | solution.py:346
  323.5 0.3 reshape.345
  323.9 0.8 reduce_sum.19
  324.7 2.8 slice_reduce_fusion.3
  327.5 0.3 copy.112
  327.8 0.1 reshape.346
  328.0 59.6 %psum.7 = f32[32,32]{1,0:T(8,128)S(1)} all-reduce(f32[32,32]{1,0:T(8,128)S(1)} %reshape.346), channel_id=1, replica_groups=mesh['groups'=2,'brick'=16] {'brick'}, use_global_device_ids=true, to_apply=%region_4.5 | all-reduce | flops 1024 | bytes 8192 | tf_op jit(solution)/shard_map/psum | solution.py:511
  387.6 0.6 broadcast_multiply_fusion.2
  388.2 0.3 convolution_convert_fusion
  388.6 0.8 copy.120
  (29 shorter events, 0.2 us)
Async XLA Ops:
  0.6 71.0 %copy-start.7 = (f32[32,32]{1,0:T(8,128)S(1)}, f32[32,32]{1,0:T(8,128)}, u32[]{:S(2)}) copy-start(f32[32,32]{1,0:T(8,128)} %param.25) | copy-start | bytes 12292
  0.6 73.5 %copy-start.5 = (f32[32,32,2,64]{3,2,1,0:T(2,128)S(1)}, f32[32,32,2,64]{3,2,1,0:T(2,128)}, u32[]{:S(2)}) copy-start(f32[32,32,2,64]{3,2,1,0:T(2,128)} %param.24) | copy-start | bytes 1572868
  7.1 100.8 %copy-start.8 = (bf16[32,32]{1,0:T(8,128)(2,1)S(1)}, bf16[32,32]{1,0:T(8,128)(2,1)}, u32[]{:S(2)}) copy-start(bf16[32,32]{1,0:T(8,128)(2,1)} %param.26) | copy-start | bytes 6148
  38.4 1.0 copy-start
  67.2 27.5 %all-to-all-start.1 = ((bf16[16,16,2048]{2,1,0:T(8,128)(2,1)}), bf16[16,16,2048]{2,1,0:T(8,128)(2,1)S(1)}, u32[]{:S(2)}, u32[]{:S(2)}) async-start(bf16[16,16,2048]{2,1,0:T(8,128)(2,1)} %bitcast.69), calls=%async_computation.1 | async-start | bytes 2097152 | tf_op jit(solution)/shard_map/all_to_all | solution.py:346
  94.7 1.0 copy-start.3
  101.3 29.8 %all-to-all-start.2 = ((bf16[16,16,2048]{2,1,0:T(8,128)(2,1)}), bf16[16,16,2048]{2,1,0:T(8,128)(2,1)S(1)}, u32[]{:S(2)}, u32[]{:S(2)}) async-start(bf16[16,16,2048]{2,1,0:T(8,128)(2,1)} %bitcast.71), calls=%async_computation.2 | async-start | bytes 2097152 | tf_op jit(solution)/shard_map/all_to_all | solution.py:346
  131.1 1.0 copy-start.4
  225.0 29.8 %all-to-all-start.3 = ((bf16[16,16,2048]{2,1,0:T(8,128)(2,1)}), bf16[16,16,2048]{2,1,0:T(8,128)(2,1)S(1)}, u32[]{:S(2)}, u32[]{:S(2)}) async-start(bf16[16,16,2048]{2,1,0:T(8,128)(2,1)} %bitcast.68), calls=%async_computation.3 | async-start | bytes 2097152 | tf_op jit(solution)/shard_map/all_to_all | solution.py:346
  254.8 1.1 copy-start.2
  262.1 61.4 %copy-start.6 = (f32[512,128]{1,0:T(8,128)S(1)}, f32[512,128]{1,0:T(8,128)}, u32[]{:S(2)}) copy-start(f32[512,128]{1,0:T(8,128)} %get-tuple-element.20) | copy-start | bytes 786436
  262.1 29.9 %all-to-all-start.4 = ((bf16[16,16,2048]{2,1,0:T(8,128)(2,1)}), bf16[16,16,2048]{2,1,0:T(8,128)(2,1)S(1)}, u32[]{:S(2)}, u32[]{:S(2)}) async-start(bf16[16,16,2048]{2,1,0:T(8,128)(2,1)} %bitcast.70), calls=%async_computation.4 | async-start | bytes 2097152 | tf_op jit(solution)/shard_map/all_to_all | solution.py:346
  292.0 1.1 copy-start.1
  316.8 71.4 %all-to-all-start.5 = ((bf16[96,32,128]{2,1,0:T(8,128)(2,1)}), bf16[96,32,128]{2,1,0:T(8,128)(2,1)S(1)}, u32[]{:S(2)}, u32[]{:S(2)}) async-start(bf16[96,32,128]{2,1,0:T(8,128)(2,1)} %pull.1), calls=%async_computation.5 | async-start | bytes 1572864 | tf_op jit(solution)/shard_map/all_to_all | solution.py:346

commit v2 on v1

--- a/solution.py
+++ b/solution.py
@@ -87,7 +87,7 @@
 def encode_kernel(capacity, planes, grid, base, got, z_in, y_in, encoded, y_modes, total, held):
     x = pl.program_id(0)
     channels = got.shape[1] - 8
-    line_rows = grid * channels
+    pitch = channels + 8
     modes = y_in.shape[0]
     exchange_rows = modes * planes
 
@@ -114,16 +114,20 @@
                     )
                 )
             for s in range(capacity):
-                start = pl.multiple_of(base[i * capacity + s] * channels, channels)
-                total[pl.ds(start, 4 * channels), :] += sums[s]
-
-    start = pl.multiple_of(x * line_rows, line_rows)
-    encoded[...] = total[pl.ds(start, line_rows), :].astype(BF16)
+                for j in range(4):
+                    start = pl.multiple_of((base[i * capacity + s] + j) * pitch, 8)
+                    total[pl.ds(start, channels), :] += sums[s][j * channels : (j + 1) * channels]
+
+    start = pl.multiple_of(x * (grid * pitch), 8)
+    for y in range(grid):
+        encoded[y * channels : (y + 1) * channels, :] = total[
+            pl.ds(start + y * pitch, channels), :
+        ].astype(BF16)
 
     for p in range(channels // 2):
         out = forward_lines(
-            total[pl.ds(start + 2 * p, grid, stride=channels), :],
-            total[pl.ds(start + 2 * p + 1, grid, stride=channels), :],
+            total[pl.ds(start + 2 * p, grid, stride=pitch), :],
+            total[pl.ds(start + 2 * p + 1, grid, stride=pitch), :],
             z_in[...],
             y_in[...],
         )
@@ -222,11 +226,13 @@
     y_modes,
     held,
     skipped,
+    pre_act,
     grads,
     held_out,
 ):
     x = pl.program_id(0)
     channels, grid = cotangent.shape[0], cotangent.shape[2]
+    pitch = channels + 8
     modes = y_in.shape[0]
     exchange_rows = modes * planes
 
@@ -235,33 +241,45 @@
         spread(got, held)
 
     for g in range(grid * channels // 256):
-        skipped[g * 256 : (g + 1) * 256, :] = dot(skip[...], encoded[g * 256 : (g + 1) * 256, :])
+        mixed = dot(skip[...], encoded[g * 256 : (g + 1) * 256, :])
+        for i in range(256 // channels):
+            y = g * (256 // channels) + i
+            skipped[y * pitch : y * pitch + channels, :] = mixed[i * channels : (i + 1) * channels]
 
     root = math.sqrt(2.0 / math.pi)
 
-    @pl.loop(0, channels // 2)
-    def _(p):
+    for p in range(channels // 2):
         values = held[pl.ds(p * exchange_rows + x, modes, stride=planes), :]
         spectral = inverse_lines(values, z_out[...], y_out[...])
-        halves = []
         for h in range(2):
             d = 2 * p + h
-            pre = spectral[:, h * 128 : (h + 1) * 128] + skipped[pl.ds(d, grid, stride=channels), :]
-            square = pre * pre
-            turned = jnp.tanh(pre * (root + (root * 0.044715) * square))
-            gate = 0.5 + 0.5 * turned
-            latent[d, 0] = (pre * gate).astype(BF16)
-            slope = gate + (0.5 * pre) * (1.0 - turned * turned) * (
-                root + (root * 3.0 * 0.044715) * square
-            )
-            grad = cotangent[d, 0].astype(F32) * slope
-            grads[pl.ds(d, grid, stride=channels), :] = grad
-            halves.append(grad)
+            mixed = skipped[pl.ds(d, grid, stride=pitch), :]
+            pre_act[d] = spectral[:, h * 128 : (h + 1) * 128] + mixed
+
+    @pl.loop(0, channels, unroll=2)
+    def _(d):
+        pre = pre_act[d]
+        square = pre * pre
+        turned = jnp.tanh(pre * (root + (root * 0.044715) * square))
+        gate = 0.5 + 0.5 * turned
+        latent[d, 0] = (pre * gate).astype(BF16)
+        slope = gate + (0.5 * pre) * (1.0 - turned * turned) * (
+            root + (root * 3.0 * 0.044715) * square
+        )
+        grads[pl.ds(d, grid, stride=pitch), :] = cotangent[d, 0].astype(F32) * slope
+
+    for p in range(channels // 2):
         held_out[pl.ds(p * exchange_rows + x, modes, stride=planes), :] = forward_lines(
-            halves[0], halves[1], z_in[...], y_in[...]
+            grads[pl.ds(2 * p, grid, stride=pitch), :],
+            grads[pl.ds(2 * p + 1, grid, stride=pitch), :],
+            z_in[...],
+            y_in[...],
         )
 
-    grad_rows[...] = grads[...].astype(BF16)
+    for y in range(grid):
+        grad_rows[y * channels : (y + 1) * channels, :] = grads[
+            y * pitch : y * pitch + channels, :
+        ].astype(BF16)
 
     @pl.when(x == planes - 1)
     def _():
@@ -282,6 +300,7 @@
     skip,
     z_out,
     y_out,
+    mix_parts,
     point_grads,
     held,
     rows_held,
@@ -289,6 +308,7 @@
     arrived,
 ):
     channels = point_grads.shape[1]
+    pitch = channels + 8
     exchange_rows = back.shape[0]
     modes = exchange_rows // planes
     copy = pltpu.make_async_copy(grad_rows, rows_held, arrived)
@@ -301,8 +321,8 @@
             values = held[pl.ds(p * exchange_rows + x, modes, stride=planes), :]
             lines = inverse_lines(values, z_out[...], y_out[...])
             for h in range(2):
-                start = x * (grid * channels) + 2 * p + h
-                total[pl.ds(start, grid, stride=channels), :] = lines[:, h * 128 : (h + 1) * 128]
+                start = x * (grid * pitch) + 2 * p + h
+                total[pl.ds(start, grid, stride=pitch), :] = lines[:, h * 128 : (h + 1) * 128]
 
     copy.wait()
 
@@ -310,14 +330,22 @@
     def _(i):
         for s in range(capacity):
             block = got[i * capacity + s].astype(F32)
-            start = pl.multiple_of(base[i * capacity + s] * channels, channels)
-            span = pl.ds(start, 4 * channels)
-            rows = total[span, :] + dot(skip[...], rows_held[span, :])
+            first = base[i * capacity + s]
+            lines = jnp.concatenate(
+                [
+                    total[pl.ds(pl.multiple_of((first + j) * pitch, 8), channels), :]
+                    for j in range(4)
+                ],
+                axis=0,
+            )
+            span = pl.ds(pl.multiple_of(first * channels, channels), 4 * channels)
+            rows = lines + dot(skip[...], rows_held[span, :])
             near = dot(rows.astype(BF16), near_line_of(block, grid))
             summed = jnp.zeros((channels, 128), F32)
             for j, weight in enumerate(near_rows(block)):
                 summed += near[j * channels : (j + 1) * channels] * weight
-            point_grads[i * capacity + s] = summed.astype(BF16)
+            point_grads[i * (capacity + 1) + s] = summed.astype(BF16)
+        point_grads[i * (capacity + 1) + capacity] = mix_parts[...]
 
 
 def vmem():
@@ -367,6 +395,7 @@
     width = channels * 2 * mode_count
     exchange_rows = mode_count * planes
     line_rows = grid * channels
+    pitch = channels + 8
     pairs = channels // 2
     z_in, y_in, z_out, y_out, x_in, x_out = tables(grid, mode_count, bricks, planes, own_modes)
     share = 1.0 / (grid * grid * grid)
@@ -416,7 +445,7 @@
             jax.ShapeDtypeStruct((exchange_rows, width), BF16),
         ],
         scratch_shapes=[
-            pltpu.VMEM((planes * line_rows, 128), F32),
+            pltpu.VMEM((planes * grid * pitch, 128), F32),
             pltpu.VMEM((pairs * exchange_rows, 128), F32),
         ],
         compiler_params=params(),
@@ -463,8 +492,9 @@
         ],
         scratch_shapes=[
             pltpu.VMEM((pairs * exchange_rows, 128), F32),
-            pltpu.VMEM((line_rows, 128), F32),
-            pltpu.VMEM((line_rows, 128), F32),
+            pltpu.VMEM((grid * pitch, 128), F32),
+            pltpu.VMEM((channels, grid, 128), F32),
+            pltpu.VMEM((grid * pitch, 128), F32),
             pltpu.VMEM((pairs * exchange_rows, 128), F32),
         ],
         compiler_params=params(),
@@ -508,17 +538,23 @@
         axis=2,
     )
     local_mix = by_part.transpose(1, 3, 0, 2).reshape(channels, channels)
-    mix_grads = lax.psum(local_mix, "brick") / grid
+    flat_mix = local_mix.reshape(-1, 128)
+    first_part = head(flat_mix)
+    second_part = head(flat_mix - first_part)
+    third_part = flat_mix - first_part - second_part
+    mix_parts = jnp.concatenate([first_part, second_part, third_part], axis=0).astype(BF16)
+    mix_rows = flat_mix.shape[0]
+    mix_parts = jnp.pad(mix_parts, ((0, channels - 3 * mix_rows), (0, 0)))
 
     pulled = pl.pallas_call(
         lambda *refs: pull_kernel(capacity, planes, grid, *refs),
-        in_specs=[smem, vmem(), vmem(), pl.BlockSpec(memory_space=pl.ANY)] + [vmem()] * 3,
+        in_specs=[smem, vmem(), vmem(), pl.BlockSpec(memory_space=pl.ANY)] + [vmem()] * 4,
         out_specs=vmem(),
-        out_shape=jax.ShapeDtypeStruct((slots, channels, 128), BF16),
+        out_shape=jax.ShapeDtypeStruct((slots + bricks, channels, 128), BF16),
         scratch_shapes=[
             pltpu.VMEM((pairs * exchange_rows, 128), F32),
             pltpu.VMEM((planes * line_rows, 128), BF16),
-            pltpu.VMEM((planes * line_rows, 128), F32),
+            pltpu.VMEM((planes * grid * pitch, 128), F32),
             pltpu.SemaphoreType.DMA,
         ],
         compiler_params=params(),
@@ -531,8 +567,12 @@
         jnp.kron(eye4, skip_weight.T),
         table(z_out),
         table(y_out),
-    )
-    returned = exchange(pulled)
+        mix_parts,
+    )
+    returned = exchange(pulled).reshape(bricks, capacity + 1, channels, 128)
+    shares = returned[:, capacity, : 3 * mix_rows].astype(F32).reshape(bricks, 3, mix_rows, 128)
+    mix_grads = jnp.sum(shares, axis=(0, 1)).reshape(channels, channels) / grid
+    returned = returned[:, :capacity].reshape(slots, channels, 128)
     point_grads = jnp.einsum("sb,scp->cbp", chosen, returned, preferred_element_type=F32)
     return (latent_grid, point_grads.astype(BF16).reshape(channels, points), mix_grads)
 

time: 395 us -> 288 us (0.73); the launches traced: 389 us -> 287 us
  Pallas kernels: 156 us -> 95.2 us
  blocking collectives: 90.8 us -> 60.8 us
  starting transfers between devices: 31.3 us -> 24.4 us
  waiting for transfers between devices: 83.5 us -> 77.4 us
    psum x1 -> x0, blocking collectives: 59.6 us -> none  [shards(): mix_grads = lax.psum(local_mix, 'brick') / grid]
    pallas_call x1, Pallas kernels: 92.9 us -> 41.9 us  [shards(): pl.pallas_call(lambda *refs: layer_kernel(planes, *refs), grid=(planes,),...]
    all_to_all x1 -> x2, blocking collectives: 31.2 us -> 60.8 us  [exchange(): lax.all_to_all(values, 'brick', split_axis=0, concat_axis=0, tiled=True)]
    pallas_call x1, Pallas kernels: 23.7 us -> 15.8 us  [shards(): pl.pallas_call(lambda *refs: pull_kernel(capacity, planes, grid, *refs),...]
    all_to_all x5 -> x4, starting transfers between devices: 31.3 us -> 24.4 us  [exchange(): lax.all_to_all(values, 'brick', split_axis=0, concat_axis=0, tiled=True)]
    all_to_all x5 -> x4, waiting for transfers between devices: 83.5 us -> 77.4 us  [exchange(): lax.all_to_all(values, 'brick', split_axis=0, concat_axis=0, tiled=True)]
  transfers between devices with their start and end apart: 5 -> 4, of which waited for: 4 -> 4; matrix products, arithmetic and copies ran while one was open for 4% -> 5% of each run, Pallas kernels for 0% -> 0%
where the time goes in v2:
time: 288 us; the launch traced here: 287 us
  Pallas kernels  95.2 us (33%)
  waiting for transfers between devices  77.4 us (27%)
  blocking collectives  60.8 us (21%)
  starting transfers between devices  24.4 us (8%)
  local copies, waits for them, and re-layouts  21.4 us (7%)
  other arithmetic  6.14 us (2%)
    all_to_all x4, waiting for transfers between devices, exchange(): lax.all_to_all(values, 'brick', split_axis=0, concat_axis=0, tiled=True)  77.4 us
    all_to_all x2, blocking collectives, exchange(): lax.all_to_all(values, 'brick', split_axis=0, concat_axis=0, tiled=True)  60.8 us
    pallas_call x1, Pallas kernels, shards(): pl.pallas_call(lambda *refs: layer_kernel(planes, *refs), grid=(planes,),...  41.9 us
    pallas_call x1, Pallas kernels, shards(): pl.pallas_call(lambda *refs: encode_kernel(capacity, planes, grid, *refs)...  25.7 us
    all_to_all x4, starting transfers between devices, exchange(): lax.all_to_all(values, 'brick', split_axis=0, concat_axis=0, tiled=True)  24.4 us
    pallas_call x1, Pallas kernels, shards(): pl.pallas_call(lambda *refs: pull_kernel(capacity, planes, grid, *refs),...  15.8 us
    pallas_call x1, Pallas kernels, shards(): pl.pallas_call(middle_grad_kernel, in_specs=[vmem()] * 6, out_specs=[vmem...  6.22 us
    unnamed x19, local copies, waits for them, and re-layouts  6.03 us
  transfers between devices with their start and end apart: 4, of which 4 were waited for; matrix products, arithmetic and copies ran while one was open for 5% of the time, Pallas kernels for 0%

profile of v2, /device:TPU:1, one launch (start us, length us, event | category | flops | bytes accessed | tf_op | source)
XLA Modules:
  0.0 287.2 jit_solution(9292321140821343027)
XLA Ops:
  0.7 0.8 fusion.10
  1.5 0.8 select_reduce_fusion
  2.4 1.0 fusion.23
  3.4 1.0 copy.123
  4.4 0.7 reduce_min.9
  5.1 0.7 add_convert_fusion
  5.8 0.1 constant_dynamic-update-slice_fusion.7
  5.9 0.1 constant_dynamic-update-slice_fusion.6
  5.9 0.1 constant_dynamic-update-slice_fusion.5
  6.0 0.1 constant_dynamic-update-slice_fusion.4
  6.1 0.1 constant_dynamic-update-slice_fusion
  6.2 0.5 fusion.13
  6.8 0.4 copy.129
  7.2 31.2 %all_to_all.54.refs_1_ = bf16[96,40,128]{2,1,0:T(8,128)(2,1)S(1)} all-to-all(bf16[96,40,128]{2,1,0:T(8,128)(2,1)S(1)} %copy.129), channel_id=1, replica_groups=mesh['groups'=2,'brick'=16] {'brick'}, dimensions={0} | all-to-all | bytes 1966080 | tf_op jit(solution)/shard_map/all_to_all | solution.py:374
  38.4 0.8 fusion.2.refs_0_
  39.2 0.1 copy-done
  39.3 25.7 %encode.1 = (bf16[32768,128]{1,0:T(8,128)(2,1)}, bf16[256,2048]{1,0:T(8,128)(2,1)}) custom-call(s32[96]{0:T(128)} %fusion.2.refs_0_, bf16[96,40,128]{2,1,0:T(8,128)(2,1)} %copy-done, bf16[256,256]{1,0:T(8,128)(2,1)} %constant.67.clone.refs_2_, bf16[32,256]{1,0:T(8,128)(2,1)} %constant.68.clone.refs_3_.refs_7_), custom_call_target="tpu_custom_call" | custom-call | tf_op jit(solution)/shard_map/encode/pallas_call | solution.py:435
  65.0 4.4 %all-to-all-start.1 = ((bf16[16,16,2048]{2,1,0:T(8,128)(2,1)}), bf16[16,16,2048]{2,1,0:T(8,128)(2,1)S(1)}, u32[]{:S(2)}, u32[]{:S(2)}) async-start(bf16[16,16,2048]{2,1,0:T(8,128)(2,1)} %bitcast.77), calls=%async_computation.1 | async-start | bytes 2097152 | tf_op jit(solution)/shard_map/all_to_all | solution.py:374
  69.4 0.2 reshape.347
  69.6 0.3 slice_reduce_fusion.11
  69.9 0.1 copy.115
  70.0 0.3 copy.116
  70.4 0.6 broadcast_in_dim.50
  71.0 1.0 reshape.349.weights
  72.0 0.6 copy.114
  72.6 1.2 reshape.346.scale
  73.8 18.8 %all-to-all-done.1 = bf16[16,16,2048]{2,1,0:T(8,128)(2,1)S(1)} async-done(((bf16[16,16,2048]{2,1,0:T(8,128)(2,1)}), bf16[16,16,2048]{2,1,0:T(8,128)(2,1)S(1)}, u32[]{:S(2)}, u32[]{:S(2)}) %all-to-all-start.1) | async-done | bytes 1048608 | tf_op jit(solution)/shard_map/all_to_all | solution.py:374
  92.6 1.0 copy-done.3
  93.5 5.5 %middle.1 = (f32[64,2048]{1,0:T(8,128)}, bf16[256,2048]{1,0:T(8,128)(2,1)}) custom-call(bf16[256,2048]{1,0:T(8,128)(2,1)} %bitcast.69, bf16[128,256]{1,0:T(8,128)(2,1)} %constant.69.clone.x_in, bf16[256,128]{1,0:T(8,128)(2,1)} %constant.70.clone.x_out, f32[64,2048]{1,0:T(8,128)} %reshape.346.scale, f32[16,32,128]{2,1,0:T(8,128)} %reshape.349.weights), custom_call_target="tpu_custom_call" | custom-call | tf_op jit(solution)/shard_map/middle/pallas_call | solution.py:457
  99.1 6.7 %all-to-all-start.2 = ((bf16[16,16,2048]{2,1,0:T(8,128)(2,1)}), bf16[16,16,2048]{2,1,0:T(8,128)(2,1)S(1)}, u32[]{:S(2)}, u32[]{:S(2)}) async-start(bf16[16,16,2048]{2,1,0:T(8,128)(2,1)} %bitcast.78), calls=%async_computation.2 | async-start | bytes 2097152 | tf_op jit(solution)/shard_map/all_to_all | solution.py:374
  105.8 0.1 broadcast_multiply_fusion
  105.9 1.0 mul.80.refs_3_
  106.9 22.0 %all-to-all-done.2 = bf16[16,16,2048]{2,1,0:T(8,128)(2,1)S(1)} async-done(((bf16[16,16,2048]{2,1,0:T(8,128)(2,1)}), bf16[16,16,2048]{2,1,0:T(8,128)(2,1)S(1)}, u32[]{:S(2)}, u32[]{:S(2)}) %all-to-all-start.2) | async-done | bytes 1048608 | tf_op jit(solution)/shard_map/all_to_all | solution.py:374
  128.9 1.0 copy-done.4
  129.9 41.9 %layer.1 = (bf16[32,8,128,128]{3,2,1,0:T(8,128)(2,1)}, bf16[32768,128]{1,0:T(8,128)(2,1)}, bf16[256,2048]{1,0:T(8,128)(2,1)}) custom-call(bf16[256,2048]{1,0:T(8,128)(2,1)} %bitcast.70, bf16[32768,128]{1,0:T(8,128)(2,1)} %get-tuple-element.14.refs_1_, bf16[32,8,128,128]{3,2,1,0:T(8,128)(2,1)} %refs_2_.2, bf16[256,256]{1,0:T(8,128)(2,1)} %mul.80.refs_3_, ...), custom_call_target="tpu_custom_call" | custom-call | tf_op jit(solution)/shard_map/layer/pallas_call | solution.py:474
  171.7 6.7 %all-to-all-start.3 = ((bf16[16,16,2048]{2,1,0:T(8,128)(2,1)}), bf16[16,16,2048]{2,1,0:T(8,128)(2,1)S(1)}, u32[]{:S(2)}, u32[]{:S(2)}) async-start(bf16[16,16,2048]{2,1,0:T(8,128)(2,1)} %bitcast.76), calls=%async_computation.3 | async-start | bytes 2097152 | tf_op jit(solution)/shard_map/all_to_all | solution.py:374
  178.4 0.1 copy.117
  178.5 0.2 reshape.350
  178.7 0.3 slice_reduce_fusion.7
  179.0 0.1 copy.118
  179.1 0.3 copy.119
  179.4 0.6 broadcast_in_dim.51
  180.1 1.0 reshape.352.weights
  181.1 20.5 %all-to-all-done.3 = bf16[16,16,2048]{2,1,0:T(8,128)(2,1)S(1)} async-done(((bf16[16,16,2048]{2,1,0:T(8,128)(2,1)}), bf16[16,16,2048]{2,1,0:T(8,128)(2,1)S(1)}, u32[]{:S(2)}, u32[]{:S(2)}) %all-to-all-start.3) | async-done | bytes 1048608 | tf_op jit(solution)/shard_map/all_to_all | solution.py:374
  201.6 1.1 copy-done.2
  202.6 6.2 %middle_grad.1 = (bf16[256,2048]{1,0:T(8,128)(2,1)}, f32[512,128]{1,0:T(8,128)}) custom-call(bf16[256,2048]{1,0:T(8,128)(2,1)} %bitcast.68, bf16[128,256]{1,0:T(8,128)(2,1)} %constant.69.clone.x_in, bf16[256,128]{1,0:T(8,128)(2,1)} %constant.70.clone.x_out, f32[64,2048]{1,0:T(8,128)} %reshape.346.scale, f32[16,32,128]{2,1,0:T(8,128)} %reshape.352.weights, ...), custom_call_target="tpu_custom_call" | custom-call | tf_op jit(solution)/shard_map/middle_grad/pallas_call | solution.py:513
  208.9 6.7 %all-to-all-start.4 = ((bf16[16,16,2048]{2,1,0:T(8,128)(2,1)}), bf16[16,16,2048]{2,1,0:T(8,128)(2,1)S(1)}, u32[]{:S(2)}, u32[]{:S(2)}) async-start(bf16[16,16,2048]{2,1,0:T(8,128)(2,1)} %bitcast.75), calls=%async_computation.4 | async-start | bytes 2097152 | tf_op jit(solution)/shard_map/all_to_all | solution.py:374
  215.5 0.1 copy.120
  215.6 0.1 broadcast_multiply_fusion.1
  215.8 0.7 mul.84.refs_4_
  216.5 1.3 reshape.353
  217.8 0.8 reduce_sum.35
  218.6 2.8 slice_reduce_fusion.3
  221.4 0.3 copy.121
  221.8 0.2 reshape_reshape.3
  221.9 0.6 fusion.16.refs_7_
  222.5 16.1 %all-to-all-done.4 = bf16[16,16,2048]{2,1,0:T(8,128)(2,1)S(1)} async-done(((bf16[16,16,2048]{2,1,0:T(8,128)(2,1)}), bf16[16,16,2048]{2,1,0:T(8,128)(2,1)S(1)}, u32[]{:S(2)}, u32[]{:S(2)}) %all-to-all-start.4) | async-done | bytes 1048608 | tf_op jit(solution)/shard_map/all_to_all | solution.py:374
  238.7 1.1 copy-done.1
  239.7 15.8 %pull.1 = bf16[112,32,128]{2,1,0:T(8,128)(2,1)} custom-call(s32[96]{0:T(128)} %fusion.2.refs_0_, bf16[96,40,128]{2,1,0:T(8,128)(2,1)} %copy-done, bf16[256,2048]{1,0:T(8,128)(2,1)} %bitcast.67, bf16[32768,128]{1,0:T(8,128)(2,1)} %get-tuple-element.19.refs_3_, bf16[128,128]{1,0:T(8,128)(2,1)} %mul.84.refs_4_, bf16[128,512]{1,0:T(8,128)(2,1)} %constant.74.clone.refs_5_, ...), custom_call_target="tpu_custom_call" | custom-call | tf_op jit(solution)/shard_map/pull/pallas_call | solution.py:549
  255.6 29.6 %all_to_all.55 = bf16[112,32,128]{2,1,0:T(8,128)(2,1)S(1)} all-to-all(bf16[112,32,128]{2,1,0:T(8,128)(2,1)} %pull.1), channel_id=1, replica_groups=mesh['groups'=2,'brick'=16] {'brick'}, dimensions={0} | all-to-all | bytes 1835008 | tf_op jit(solution)/shard_map/all_to_all | solution.py:374
  285.2 0.1 slice.99
  285.3 0.3 convolution_convert_fusion
  285.7 0.8 copy.130
  286.5 0.7 div.26
  (31 shorter events, 0.3 us)
Async XLA Ops:
  0.6 68.8 %copy-start.6 = (f32[32,32]{1,0:T(8,128)S(1)}, f32[32,32]{1,0:T(8,128)}, u32[]{:S(2)}) copy-start(f32[32,32]{1,0:T(8,128)} %param.25) | copy-start | bytes 12292
  0.6 71.3 %copy-start.5 = (f32[32,32,2,64]{3,2,1,0:T(2,128)S(1)}, f32[32,32,2,64]{3,2,1,0:T(2,128)}, u32[]{:S(2)}) copy-start(f32[32,32,2,64]{3,2,1,0:T(2,128)} %param.24) | copy-start | bytes 1572868
  7.1 98.6 %copy-start.7 = (bf16[32,32]{1,0:T(8,128)(2,1)S(1)}, bf16[32,32]{1,0:T(8,128)(2,1)}, u32[]{:S(2)}) copy-start(bf16[32,32]{1,0:T(8,128)(2,1)} %param.26) | copy-start | bytes 6148
  38.4 1.0 copy-start
  65.0 27.5 %all-to-all-start.1 = ((bf16[16,16,2048]{2,1,0:T(8,128)(2,1)}), bf16[16,16,2048]{2,1,0:T(8,128)(2,1)S(1)}, u32[]{:S(2)}, u32[]{:S(2)}) async-start(bf16[16,16,2048]{2,1,0:T(8,128)(2,1)} %bitcast.77), calls=%async_computation.1 | async-start | bytes 2097152 | tf_op jit(solution)/shard_map/all_to_all | solution.py:374
  92.6 1.0 copy-start.3
  99.1 29.8 %all-to-all-start.2 = ((bf16[16,16,2048]{2,1,0:T(8,128)(2,1)}), bf16[16,16,2048]{2,1,0:T(8,128)(2,1)S(1)}, u32[]{:S(2)}, u32[]{:S(2)}) async-start(bf16[16,16,2048]{2,1,0:T(8,128)(2,1)} %bitcast.78), calls=%async_computation.2 | async-start | bytes 2097152 | tf_op jit(solution)/shard_map/all_to_all | solution.py:374
  128.9 1.0 copy-start.4
  171.7 29.8 %all-to-all-start.3 = ((bf16[16,16,2048]{2,1,0:T(8,128)(2,1)}), bf16[16,16,2048]{2,1,0:T(8,128)(2,1)S(1)}, u32[]{:S(2)}, u32[]{:S(2)}) async-start(bf16[16,16,2048]{2,1,0:T(8,128)(2,1)} %bitcast.76), calls=%async_computation.3 | async-start | bytes 2097152 | tf_op jit(solution)/shard_map/all_to_all | solution.py:374
  201.6 1.1 copy-start.2
  208.9 29.8 %all-to-all-start.4 = ((bf16[16,16,2048]{2,1,0:T(8,128)(2,1)}), bf16[16,16,2048]{2,1,0:T(8,128)(2,1)S(1)}, u32[]{:S(2)}, u32[]{:S(2)}) async-start(bf16[16,16,2048]{2,1,0:T(8,128)(2,1)} %bitcast.75), calls=%async_computation.4 | async-start | bytes 2097152 | tf_op jit(solution)/shard_map/all_to_all | solution.py:374
  238.7 1.1 copy-start.1

commit v3 on v2

--- a/solution.py
+++ b/solution.py
@@ -11,6 +11,7 @@
 F32 = jnp.float32
 BF16 = jnp.bfloat16
 VMEM_BYTES = 56 * 1024 * 1024
+PARTS = 2
 
 
 def rounded(values):
@@ -43,10 +44,12 @@
         x_in[1, k, :, :, k, :] = by_brick_sin.transpose(2, 0, 1)
         x_out[:, k, :, 0, k, :] = by_brick_cos
         x_out[:, k, :, 1, k, :] = -by_brick_sin
-    rows = bricks * own_modes * planes
-    x_in = x_in.reshape(2 * own_modes * modes, rows)
-    x_out = x_out.reshape(rows, 2 * own_modes * modes)
-    return z_in, y_in, z_out, y_out, x_in, x_out
+    part = planes // PARTS
+    cuts = [slice(h * part, (h + 1) * part) for h in range(PARTS)]
+    x_out_parts = [x_out[:, :, cut].reshape(-1, 2 * own_modes * modes) for cut in cuts]
+    x_in_parts = [x_in[..., cut].reshape(2 * own_modes * modes, -1) for cut in cuts]
+    return (z_in, y_in, z_out, y_out, x_in.reshape(2 * own_modes * modes, -1), x_in_parts, x_out_parts,
+            x_out.reshape(-1, 2 * own_modes * modes))
 
 
 def dot(left, right):
@@ -141,10 +144,10 @@
             ].astype(BF16)
 
 
-def x_forward(got, x_in, even, rows):
-    both = dot(x_in[...], got[...])
+def x_forward(gots, tables_in, even, rows):
+    both = sum(dot(x_in[...], got[...]) for got, x_in in zip(gots, tables_in))
     parts = []
-    for p in range(got.shape[1] // 128):
+    for p in range(both.shape[1] // 128):
         span = slice(p * 128, (p + 1) * 128)
         parts.append(both[:rows, span] + rotate(both[rows:, span], even))
     return parts
@@ -164,11 +167,14 @@
     return total
 
 
-def middle_kernel(got, x_in, x_out, scale, weights, scaled, back, straight, swapped):
+def middle_kernel(got, x_in, *refs):
+    x_outs, refs = refs[:PARTS], refs[PARTS:]
+    scale, weights, scaled = refs[:3]
+    backs, (straight, swapped) = refs[3 : 3 + PARTS], refs[3 + PARTS :]
     rows = scale.shape[0]
     pairs = got.shape[1] // 128
     even = is_even((rows, 128))
-    for p, modes in enumerate(x_forward(got, x_in, even, rows)):
+    for p, modes in enumerate(x_forward([got], [x_in], even, rows)):
         span = slice(p * 128, (p + 1) * 128)
         real, imag = scale_parts(scale[:, span], even)
         value = modes * real - rotate(modes, even) * imag
@@ -178,16 +184,17 @@
     for d in range(pairs):
         mixed = mix_pairs(d, weights, straight, swapped, pairs)
         stacked = jnp.concatenate([mixed, rotate(mixed, even)], axis=0).astype(BF16)
-        back[:, d * 128 : (d + 1) * 128] = dot(x_out[...], stacked).astype(BF16)
-
-
-def middle_grad_kernel(
-    got, x_in, x_out, scale, weights, scaled, back, products, straight, swapped
-):
+        for back, x_out in zip(backs, x_outs):
+            back[:, d * 128 : (d + 1) * 128] = dot(x_out[...], stacked).astype(BF16)
+
+
+def middle_grad_kernel(*refs):
+    gots, x_ins, refs = refs[:PARTS], refs[PARTS : 2 * PARTS], refs[2 * PARTS :]
+    x_out, scale, weights, scaled, back, products, straight, swapped = refs
     rows = scale.shape[0]
-    pairs = got.shape[1] // 128
+    pairs = scale.shape[1] // 128
     even = is_even((rows, 128))
-    for p, grad in enumerate(x_forward(got, x_in, even, rows)):
+    for p, grad in enumerate(x_forward(gots, x_ins, even, rows)):
         straight[p] = grad
         swapped[p] = pltpu.roll(grad, 64, 1)
     for c in range(pairs):
@@ -221,6 +228,7 @@
     y_out,
     z_in,
     y_in,
+    _,
     latent,
     grad_rows,
     y_modes,
@@ -296,23 +304,27 @@
     base,
     got,
     back,
-    grad_rows,
     skip,
     z_out,
     y_out,
     mix_parts,
-    point_grads,
-    held,
-    rows_held,
-    total,
-    arrived,
+    *refs,
 ):
+    grad_rows, refs = refs[:PARTS], refs[PARTS:]
+    point_grads, held, rows_held, total, arrived = refs
     channels = point_grads.shape[1]
     pitch = channels + 8
     exchange_rows = back.shape[0]
     modes = exchange_rows // planes
-    copy = pltpu.make_async_copy(grad_rows, rows_held, arrived)
-    copy.start()
+    part_rows = rows_held.shape[0] // PARTS
+    copies = [
+        pltpu.make_async_copy(
+            part, rows_held.at[h * part_rows : (h + 1) * part_rows], arrived.at[h]
+        )
+        for h, part in enumerate(grad_rows)
+    ]
+    for copy in copies:
+        copy.start()
     spread(back, held)
 
     @pl.loop(0, planes)
@@ -324,7 +336,8 @@
                 start = x * (grid * pitch) + 2 * p + h
                 total[pl.ds(start, grid, stride=pitch), :] = lines[:, h * 128 : (h + 1) * 128]
 
-    copy.wait()
+    for copy in copies:
+        copy.wait()
 
     @pl.loop(0, got.shape[0] // capacity)
     def _(i):
@@ -397,7 +410,7 @@
     line_rows = grid * channels
     pitch = channels + 8
     pairs = channels // 2
-    z_in, y_in, z_out, y_out, x_in, x_out = tables(grid, mode_count, bricks, planes, own_modes)
+    z_in, y_in, z_out, y_out, x_in, x_in_parts, x_out_parts, x_out = tables(grid, mode_count, bricks, planes, own_modes)
     share = 1.0 / (grid * grid * grid)
 
     member = (owner_brick[:, None] == jnp.arange(bricks, dtype=jnp.int32)[None, :]).astype(
@@ -454,65 +467,90 @@
 
     scale = mode_scale.transpose(2, 1, 0, 3).reshape(own_modes * mode_count, width)
     held_modes = pltpu.VMEM((pairs, own_modes * mode_count, 128), F32)
-    scaled, back = pl.pallas_call(
+    part_rows = exchange_rows // PARTS
+    half_modes = jax.ShapeDtypeStruct((part_rows, width), BF16)
+    scaled, *backs = pl.pallas_call(
         middle_kernel,
-        in_specs=[vmem()] * 5,
-        out_specs=[vmem()] * 2,
-        out_shape=[
-            jax.ShapeDtypeStruct(scale.shape, F32),
-            jax.ShapeDtypeStruct((exchange_rows, width), BF16),
-        ],
+        in_specs=[vmem()] * (4 + PARTS),
+        out_specs=[vmem()] * (1 + PARTS),
+        out_shape=[jax.ShapeDtypeStruct(scale.shape, F32)] + [half_modes] * PARTS,
         scratch_shapes=[held_modes, held_modes],
         compiler_params=params(),
         name="middle",
-    )(exchange(y_modes), table(x_in), table(x_out), scale, pair_weights(channel_mix))
+    )(
+        exchange(y_modes),
+        table(x_in),
+        *[table(values) for values in x_out_parts],
+        scale,
+        pair_weights(channel_mix),
+    )
 
     eye8 = jnp.eye(256 // channels, dtype=BF16)
     eye4 = jnp.eye(4, dtype=BF16)
-    planes_spec = pl.BlockSpec((channels, 1, grid, grid), lambda x: (0, x, 0, 0))
-    rows_spec = pl.BlockSpec((line_rows, 128), lambda x: (x, 0))
-    latent_grid, grad_rows, grad_y_modes = pl.pallas_call(
-        lambda *refs: layer_kernel(planes, *refs),
-        grid=(planes,),
-        in_specs=[
-            whole((exchange_rows, width)),
-            rows_spec,
-            planes_spec,
-            whole((256, 256)),
-            whole(z_out.shape),
-            whole(y_out.shape),
-            whole(z_in.shape),
-            whole(y_in.shape),
-        ],
-        out_specs=[planes_spec, rows_spec, whole((exchange_rows, width))],
-        out_shape=[
-            jax.ShapeDtypeStruct(cotangent.shape, BF16),
-            jax.ShapeDtypeStruct((planes * line_rows, 128), BF16),
-            jax.ShapeDtypeStruct((exchange_rows, width), BF16),
-        ],
-        scratch_shapes=[
-            pltpu.VMEM((pairs * exchange_rows, 128), F32),
-            pltpu.VMEM((grid * pitch, 128), F32),
-            pltpu.VMEM((channels, grid, 128), F32),
-            pltpu.VMEM((grid * pitch, 128), F32),
-            pltpu.VMEM((pairs * exchange_rows, 128), F32),
-        ],
-        compiler_params=params(),
-        name="layer",
-    )(
-        exchange(back),
-        encoded,
-        cotangent,
-        jnp.kron(eye8, skip_weight),
-        table(z_out * share),
-        table(y_out),
-        table(z_in * share),
-        table(y_in),
-    )
+    part_planes = planes // PARTS
+    skip_blocks = jnp.kron(eye8, skip_weight)
+    layer_cost = pl.CostEstimate(
+        flops=40 * channels * part_planes * grid * grid,
+        bytes_accessed=16 * channels * part_planes * grid * grid,
+        transcendentals=channels * part_planes * grid * grid,
+    )
+    latent_grid = None
+    grad_rows, grad_y_modes = [], []
+    for part in range(PARTS):
+        first = part * part_planes
+        planes_spec = pl.BlockSpec(
+            (channels, 1, grid, grid), lambda x, first=first: (0, first + x, 0, 0)
+        )
+        rows_in = pl.BlockSpec((line_rows, 128), lambda x, first=first: (first + x, 0))
+        rows_out = pl.BlockSpec((line_rows, 128), lambda x: (x, 0))
+        latent_grid, rows_part, modes_part = pl.pallas_call(
+            lambda *refs: layer_kernel(part_planes, *refs),
+            grid=(part_planes,),
+            in_specs=[
+                whole((part_rows, width)),
+                rows_in,
+                planes_spec,
+                whole((256, 256)),
+                whole(z_out.shape),
+                whole(y_out.shape),
+                whole(z_in.shape),
+                whole(y_in.shape),
+                pl.BlockSpec(memory_space=pl.ANY),
+            ],
+            out_specs=[planes_spec, rows_out, whole((part_rows, width))],
+            out_shape=[
+                jax.ShapeDtypeStruct(cotangent.shape, BF16),
+                jax.ShapeDtypeStruct((part_planes * line_rows, 128), BF16),
+                half_modes,
+            ],
+            scratch_shapes=[
+                pltpu.VMEM((pairs * part_rows, 128), F32),
+                pltpu.VMEM((grid * pitch, 128), F32),
+                pltpu.VMEM((channels, grid, 128), F32),
+                pltpu.VMEM((grid * pitch, 128), F32),
+                pltpu.VMEM((pairs * part_rows, 128), F32),
+            ],
+            input_output_aliases={} if latent_grid is None else {8: 0},
+            cost_estimate=layer_cost,
+            compiler_params=params(),
+            name="layer",
+        )(
+            exchange(backs[part]),
+            encoded,
+            cotangent,
+            skip_blocks,
+            table(z_out * share),
+            table(y_out),
+            table(z_in * share),
+            table(y_in),
+            encoded if latent_grid is None else latent_grid,
+        )
+        grad_rows.append(rows_part)
+        grad_y_modes.append(modes_part)
 
     grad_back, products = pl.pallas_call(
         middle_grad_kernel,
-        in_specs=[vmem()] * 6,
+        in_specs=[vmem()] * (4 + 2 * PARTS),
         out_specs=[vmem()] * 2,
         out_shape=[
             jax.ShapeDtypeStruct((exchange_rows, width), BF16),
@@ -522,8 +560,8 @@
         compiler_params=params(),
         name="middle_grad",
     )(
-        exchange(grad_y_modes),
-        table(x_in),
+        *[exchange(values) for values in grad_y_modes],
+        *[table(values) for values in x_in_parts],
         table(x_out),
         scale,
         pair_weights(channel_mix.T),
@@ -548,14 +586,14 @@
 
     pulled = pl.pallas_call(
         lambda *refs: pull_kernel(capacity, planes, grid, *refs),
-        in_specs=[smem, vmem(), vmem(), pl.BlockSpec(memory_space=pl.ANY)] + [vmem()] * 4,
+        in_specs=[smem] + [vmem()] * 6 + [pl.BlockSpec(memory_space=pl.ANY)] * PARTS,
         out_specs=vmem(),
         out_shape=jax.ShapeDtypeStruct((slots + bricks, channels, 128), BF16),
         scratch_shapes=[
             pltpu.VMEM((pairs * exchange_rows, 128), F32),
             pltpu.VMEM((planes * line_rows, 128), BF16),
             pltpu.VMEM((planes * grid * pitch, 128), F32),
-            pltpu.SemaphoreType.DMA,
+            pltpu.SemaphoreType.DMA((PARTS,)),
         ],
         compiler_params=params(),
         name="pull",
@@ -563,11 +601,11 @@
         base,
         got,
         exchange(grad_back),
-        grad_rows,
         jnp.kron(eye4, skip_weight.T),
         table(z_out),
         table(y_out),
         mix_parts,
+        *grad_rows,
     )
     returned = exchange(pulled).reshape(bricks, capacity + 1, channels, 128)
     shares = returned[:, capacity, : 3 * mix_rows].astype(F32).reshape(bricks, 3, mix_rows, 128)

time: 288 us -> 294 us (1.021)
  blocking collectives: 60.8 us -> 102 us
  waiting for transfers between devices: 77.4 us -> 46.4 us
  starting transfers between devices: 24.4 us -> 17.9 us
    all_to_all x2 -> x4, blocking collectives: 60.8 us -> 102 us  [exchange(): lax.all_to_all(values, 'brick', split_axis=0, concat_axis=0, tiled=True)]
    all_to_all x4, waiting for transfers between devices: 77.4 us -> 46.4 us  [exchange(): lax.all_to_all(values, 'brick', split_axis=0, concat_axis=0, tiled=True)]
    all_to_all x4, starting transfers between devices: 24.4 us -> 17.9 us  [exchange(): lax.all_to_all(values, 'brick', split_axis=0, concat_axis=0, tiled=True)]
    pallas_call x3 -> x4, Pallas kernels: 53.6 us -> 56.5 us  [the longest x2 44.6 us: shards(): pl.pallas_call(lambda *refs: layer_kernel(part_planes, *refs), grid=(part...]
  transfers between devices with their start and end apart: 4 -> 4, of which waited for: 4 -> 3; matrix products, arithmetic and copies ran while one was open for 5% -> 5% of each run, Pallas kernels for 0% -> 8%
where the time goes in v3:
time: 294 us; the launch traced here: 293 us
  blocking collectives  102 us (35%)
  Pallas kernels  98.1 us (33%)
  waiting for transfers between devices  46.4 us (16%)
  local copies, waits for them, and re-layouts  20.8 us (7%)
  starting transfers between devices  17.9 us (6%)
  other arithmetic  6.16 us (2%)
    all_to_all x4, blocking collectives, exchange(): lax.all_to_all(values, 'brick', split_axis=0, concat_axis=0, tiled=True)  102 us
    all_to_all x4, waiting for transfers between devices, exchange(): lax.all_to_all(values, 'brick', split_axis=0, concat_axis=0, tiled=True)  46.4 us
    pallas_call x2, Pallas kernels, shards(): pl.pallas_call(lambda *refs: layer_kernel(part_planes, *refs), grid=(part...  44.6 us
    pallas_call x1, Pallas kernels, shards(): pl.pallas_call(lambda *refs: encode_kernel(capacity, planes, grid, *refs)...  25.7 us
    all_to_all x4, starting transfers between devices, exchange(): lax.all_to_all(values, 'brick', split_axis=0, concat_axis=0, tiled=True)  17.9 us
    pallas_call x1, Pallas kernels, shards(): pl.pallas_call(lambda *refs: pull_kernel(capacity, planes, grid, *refs),...  15.9 us
    pallas_call x1, Pallas kernels, shards(): pl.pallas_call(middle_grad_kernel, in_specs=[vmem()] * (4 + 2 * PARTS), o...  6.26 us
  transfers between devices with their start and end apart: 4, of which 3 were waited for; matrix products, arithmetic and copies ran while one was open for 5% of the time, Pallas kernels for 8%

profile of v3, /device:TPU:1, one launch (start us, length us, event | category | flops | bytes accessed | tf_op | source)
XLA Modules:
  0.0 293.0 jit_solution(5282686268821099476)
XLA Ops:
  0.7 0.8 fusion.10
  1.5 0.8 select_reduce_fusion
  2.4 1.0 fusion.23
  3.4 1.0 copy.130
  4.4 0.7 reduce_min.9
  5.1 0.7 add_convert_fusion
  5.8 0.1 constant_dynamic-update-slice_fusion.7
  5.9 0.1 constant_dynamic-update-slice_fusion.6
  5.9 0.1 constant_dynamic-update-slice_fusion.5
  6.0 0.1 constant_dynamic-update-slice_fusion.4
  6.1 0.1 constant_dynamic-update-slice_fusion
  6.2 0.5 fusion.13
  6.8 0.4 copy.136
  7.2 31.2 %all_to_all.76.refs_1_ = bf16[96,40,128]{2,1,0:T(8,128)(2,1)S(1)} all-to-all(bf16[96,40,128]{2,1,0:T(8,128)(2,1)S(1)} %copy.136), channel_id=1, replica_groups=mesh['groups'=2,'brick'=16] {'brick'}, dimensions={0} | all-to-all | bytes 1966080 | tf_op jit(solution)/shard_map/all_to_all | solution.py:387
  38.4 0.8 fusion.2.refs_0_
  39.3 25.7 %encode.1 = (bf16[32768,128]{1,0:T(8,128)(2,1)}, bf16[256,2048]{1,0:T(8,128)(2,1)}) custom-call(s32[96]{0:T(128)} %fusion.2.refs_0_, bf16[96,40,128]{2,1,0:T(8,128)(2,1)} %copy-done, bf16[256,256]{1,0:T(8,128)(2,1)} %constant.75.clone.refs_2_, bf16[32,256]{1,0:T(8,128)(2,1)} %constant.76.clone.refs_3_.refs_7_), custom_call_target="tpu_custom_call" | custom-call | tf_op jit(solution)/shard_map/encode/pallas_call | solution.py:448
  65.0 4.4 %all-to-all-start.1 = ((bf16[16,16,2048]{2,1,0:T(8,128)(2,1)}), bf16[16,16,2048]{2,1,0:T(8,128)(2,1)S(1)}, u32[]{:S(2)}, u32[]{:S(2)}) async-start(bf16[16,16,2048]{2,1,0:T(8,128)(2,1)} %bitcast.82), calls=%async_computation.1 | async-start | bytes 2097152 | tf_op jit(solution)/shard_map/all_to_all | solution.py:387
  69.4 0.2 reshape.351
  69.6 0.3 slice_reduce_fusion.11
  69.9 0.1 copy.122
  70.0 0.3 copy.123
  70.4 0.6 broadcast_in_dim.50
  71.0 1.0 reshape.353.refs_3_
  72.0 0.6 copy.121
  72.6 1.2 reshape.350.refs_2_.refs_5_
  73.8 18.8 %all-to-all-done.1 = bf16[16,16,2048]{2,1,0:T(8,128)(2,1)S(1)} async-done(((bf16[16,16,2048]{2,1,0:T(8,128)(2,1)}), bf16[16,16,2048]{2,1,0:T(8,128)(2,1)S(1)}, u32[]{:S(2)}, u32[]{:S(2)}) %all-to-all-start.1) | async-done | bytes 1048608 | tf_op jit(solution)/shard_map/all_to_all | solution.py:387
  92.6 1.0 copy-done.2
  93.5 5.7 %middle.1 = (f32[64,2048]{1,0:T(8,128)}, bf16[128,2048]{1,0:T(8,128)(2,1)}, bf16[128,2048]{1,0:T(8,128)(2,1)}) custom-call(bf16[256,2048]{1,0:T(8,128)(2,1)} %bitcast.72, bf16[128,256]{1,0:T(8,128)(2,1)} %constant.77.clone.x_in, bf16[128,128]{1,0:T(8,128)(2,1)} %constant.78.clone.refs_0_, bf16[128,128]{1,0:T(8,128)(2,1)} %constant.79.clone.refs_1_, ...), custom_call_target="tpu_custom_call" | custom-call | tf_op jit(solution)/shard_map/middle/pallas_call | solution.py:472
  99.2 20.8 %all_to_all.77 = bf16[16,8,2048]{2,1,0:T(8,128)(2,1)} all-to-all(bf16[16,8,2048]{2,1,0:T(8,128)(2,1)} %bitcast.87), channel_id=1, replica_groups=mesh['groups'=2,'brick'=16] {'brick'}, dimensions={0} | all-to-all | bytes 1048576 | tf_op jit(solution)/shard_map/all_to_all | solution.py:387
  120.0 4.5 %all-to-all-start.2 = ((bf16[16,8,2048]{2,1,0:T(8,128)(2,1)}), bf16[16,8,2048]{2,1,0:T(8,128)(2,1)S(1)}, u32[]{:S(2)}, u32[]{:S(2)}) async-start(bf16[16,8,2048]{2,1,0:T(8,128)(2,1)} %bitcast.85), calls=%async_computation.2 | async-start | bytes 1048576 | tf_op jit(solution)/shard_map/all_to_all | solution.py:387
  124.6 0.1 broadcast_multiply_fusion
  124.7 1.0 mul.80.refs_3_
  125.7 22.3 %layer.2 = (bf16[32,8,128,128]{3,2,1,0:T(8,128)(2,1)}, bf16[16384,128]{1,0:T(8,128)(2,1)}, bf16[128,2048]{1,0:T(8,128)(2,1)}) custom-call(bf16[128,2048]{1,0:T(8,128)(2,1)} %bitcast.79, bf16[32768,128]{1,0:T(8,128)(2,1)} %get-tuple-element.18.refs_1_.refs_8_, bf16[32,8,128,128]{3,2,1,0:T(8,128)(2,1)} %refs_2_.5, bf16[256,256]{1,0:T(8,128)(2,1)} %mul.80.refs_3_, ...), custom_call_target="tpu_custom_call" | custom-call | flops 83886080 | bytes 33554432 | tf_op jit(solution)/shard_map/layer/pallas_call | solution.py:506
  148.0 0.8 copy-done.4
  148.8 22.3 %layer.3 = (bf16[32,8,128,128]{3,2,1,0:T(8,128)(2,1)}, bf16[16384,128]{1,0:T(8,128)(2,1)}, bf16[128,2048]{1,0:T(8,128)(2,1)}) custom-call(bf16[128,2048]{1,0:T(8,128)(2,1)} %bitcast.78, bf16[32768,128]{1,0:T(8,128)(2,1)} %get-tuple-element.18.refs_1_.refs_8_, bf16[32,8,128,128]{3,2,1,0:T(8,128)(2,1)} %refs_2_.5, ...), custom_call_target="tpu_custom_call", output_to_operand_aliasing={{0}: (8, {})} | custom-call | flops 83886080 | bytes 33554432 | tf_op jit(solution)/shard_map/layer/pallas_call | solution.py:506
  171.1 20.2 %all_to_all.78 = bf16[16,8,2048]{2,1,0:T(8,128)(2,1)} all-to-all(bf16[16,8,2048]{2,1,0:T(8,128)(2,1)} %bitcast.86), channel_id=1, replica_groups=mesh['groups'=2,'brick'=16] {'brick'}, dimensions={0} | all-to-all | bytes 1048576 | tf_op jit(solution)/shard_map/all_to_all | solution.py:387
  191.3 4.5 %all-to-all-start.4 = ((bf16[16,8,2048]{2,1,0:T(8,128)(2,1)}), bf16[16,8,2048]{2,1,0:T(8,128)(2,1)S(1)}, u32[]{:S(2)}, u32[]{:S(2)}) async-start(bf16[16,8,2048]{2,1,0:T(8,128)(2,1)} %bitcast.16), calls=%async_computation.4 | async-start | bytes 1048576 | tf_op jit(solution)/shard_map/all_to_all | solution.py:387
  195.9 0.2 reshape.354
  196.0 0.3 slice_reduce_fusion.7
  196.4 0.1 copy.125
  196.4 0.3 copy.126
  196.8 0.6 broadcast_in_dim.51
  197.4 1.0 reshape.356.refs_6_
  198.4 11.4 %all-to-all-done.4 = bf16[16,8,2048]{2,1,0:T(8,128)(2,1)S(1)} async-done(((bf16[16,8,2048]{2,1,0:T(8,128)(2,1)}), bf16[16,8,2048]{2,1,0:T(8,128)(2,1)S(1)}, u32[]{:S(2)}, u32[]{:S(2)}) %all-to-all-start.4) | async-done | bytes 524320 | tf_op jit(solution)/shard_map/all_to_all | solution.py:387
  209.9 0.8 copy-done.3
  210.7 6.3 %middle_grad.1 = (bf16[256,2048]{1,0:T(8,128)(2,1)}, f32[512,128]{1,0:T(8,128)}) custom-call(bf16[128,2048]{1,0:T(8,128)(2,1)} %bitcast.77, bf16[128,2048]{1,0:T(8,128)(2,1)} %bitcast.76, bf16[128,128]{1,0:T(8,128)(2,1)} %constant.83.clone.refs_2_, bf16[128,128]{1,0:T(8,128)(2,1)} %constant.84.clone.refs_3_, bf16[256,128]{1,0:T(8,128)(2,1)} %constant.85.clone.refs_4_, ...), custom_call_target="tpu_custom_call" | custom-call | tf_op jit(solution)/shard_map/middle_grad/pallas_call | solution.py:551
  216.9 4.5 %all-to-all-start.6 = ((bf16[16,16,2048]{2,1,0:T(8,128)(2,1)}), bf16[16,16,2048]{2,1,0:T(8,128)(2,1)S(1)}, u32[]{:S(2)}, u32[]{:S(2)}) async-start(bf16[16,16,2048]{2,1,0:T(8,128)(2,1)} %bitcast.81), calls=%async_computation.6 | async-start | bytes 2097152 | tf_op jit(solution)/shard_map/all_to_all | solution.py:387
  221.4 0.1 copy.127
  221.5 0.1 broadcast_multiply_fusion.1
  221.7 0.7 mul.84.refs_3_
  222.4 1.3 reshape.357
  223.7 0.8 reduce_sum.35
  224.5 2.8 slice_reduce_fusion.3
  227.3 0.3 copy.128
  227.6 0.2 reshape_reshape.3
  227.8 0.6 fusion.16.refs_6_
  228.4 16.1 %all-to-all-done.6 = bf16[16,16,2048]{2,1,0:T(8,128)(2,1)S(1)} async-done(((bf16[16,16,2048]{2,1,0:T(8,128)(2,1)}), bf16[16,16,2048]{2,1,0:T(8,128)(2,1)S(1)}, u32[]{:S(2)}, u32[]{:S(2)}) %all-to-all-start.6) | async-done | bytes 1048608 | tf_op jit(solution)/shard_map/all_to_all | solution.py:387
  244.6 1.0 copy-done.1
  245.6 15.9 %pull.1 = bf16[112,32,128]{2,1,0:T(8,128)(2,1)} custom-call(s32[96]{0:T(128)} %fusion.2.refs_0_, bf16[96,40,128]{2,1,0:T(8,128)(2,1)} %copy-done, bf16[256,2048]{1,0:T(8,128)(2,1)} %bitcast.71, bf16[128,128]{1,0:T(8,128)(2,1)} %mul.84.refs_3_, bf16[128,512]{1,0:T(8,128)(2,1)} %constant.86.clone.refs_4_, bf16[128,64]{1,0:T(8,128)(2,1)} %constant.81.clone.refs_5_, ...), custom_call_target="tpu_custom_call" | custom-call | tf_op jit(solution)/shard_map/pull/pallas_call | solution.py:587
  261.5 29.6 %all_to_all.79 = bf16[112,32,128]{2,1,0:T(8,128)(2,1)S(1)} all-to-all(bf16[112,32,128]{2,1,0:T(8,128)(2,1)} %pull.1), channel_id=1, replica_groups=mesh['groups'=2,'brick'=16] {'brick'}, dimensions={0} | all-to-all | bytes 1835008 | tf_op jit(solution)/shard_map/all_to_all | solution.py:387
  291.1 0.1 slice.99
  291.2 0.3 convolution_convert_fusion
  291.5 0.8 copy.137
  292.3 0.7 div.26
  (34 shorter events, 0.4 us)
Async XLA Ops:
  0.6 68.8 %copy-start.6 = (f32[32,32]{1,0:T(8,128)S(1)}, f32[32,32]{1,0:T(8,128)}, u32[]{:S(2)}) copy-start(f32[32,32]{1,0:T(8,128)} %param.31) | copy-start | bytes 12292
  0.6 71.3 %copy-start.5 = (f32[32,32,2,64]{3,2,1,0:T(2,128)S(1)}, f32[32,32,2,64]{3,2,1,0:T(2,128)}, u32[]{:S(2)}) copy-start(f32[32,32,2,64]{3,2,1,0:T(2,128)} %param.30) | copy-start | bytes 1572868
  7.1 117.4 %copy-start.7 = (bf16[32,32]{1,0:T(8,128)(2,1)S(1)}, bf16[32,32]{1,0:T(8,128)(2,1)}, u32[]{:S(2)}) copy-start(bf16[32,32]{1,0:T(8,128)(2,1)} %param.32) | copy-start | bytes 6148
  38.4 1.0 copy-start
  65.0 27.5 %all-to-all-start.1 = ((bf16[16,16,2048]{2,1,0:T(8,128)(2,1)}), bf16[16,16,2048]{2,1,0:T(8,128)(2,1)S(1)}, u32[]{:S(2)}, u32[]{:S(2)}) async-start(bf16[16,16,2048]{2,1,0:T(8,128)(2,1)} %bitcast.82), calls=%async_computation.1 | async-start | bytes 2097152 | tf_op jit(solution)/shard_map/all_to_all | solution.py:387
  92.6 1.0 copy-start.2
  120.0 27.9 %all-to-all-start.2 = ((bf16[16,8,2048]{2,1,0:T(8,128)(2,1)}), bf16[16,8,2048]{2,1,0:T(8,128)(2,1)S(1)}, u32[]{:S(2)}, u32[]{:S(2)}) async-start(bf16[16,8,2048]{2,1,0:T(8,128)(2,1)} %bitcast.85), calls=%async_computation.2 | async-start | bytes 1048576 | tf_op jit(solution)/shard_map/all_to_all | solution.py:387
  148.0 0.8 copy-start.4
  191.3 18.6 %all-to-all-start.4 = ((bf16[16,8,2048]{2,1,0:T(8,128)(2,1)}), bf16[16,8,2048]{2,1,0:T(8,128)(2,1)S(1)}, u32[]{:S(2)}, u32[]{:S(2)}) async-start(bf16[16,8,2048]{2,1,0:T(8,128)(2,1)} %bitcast.16), calls=%async_computation.4 | async-start | bytes 1048576 | tf_op jit(solution)/shard_map/all_to_all | solution.py:387
  209.9 0.8 copy-start.3
  216.9 27.6 %all-to-all-start.6 = ((bf16[16,16,2048]{2,1,0:T(8,128)(2,1)}), bf16[16,16,2048]{2,1,0:T(8,128)(2,1)S(1)}, u32[]{:S(2)}, u32[]{:S(2)}) async-start(bf16[16,16,2048]{2,1,0:T(8,128)(2,1)} %bitcast.81), calls=%async_computation.6 | async-start | bytes 2097152 | tf_op jit(solution)/shard_map/all_to_all | solution.py:387
  244.6 1.0 copy-start.1

commit v4 on v2

--- a/solution.py
+++ b/solution.py
@@ -30,8 +30,8 @@
     turn[2 * numbers + 1, 2 * numbers] = 1.0
     turn[2 * numbers, 2 * numbers + 1] = -1.0
     two = np.eye(2, dtype=np.float32)
-    z_in = np.concatenate([np.kron(two, line), np.kron(two, line @ turn)], axis=1)
-    y_in = np.concatenate([cosine.T, sine.T], axis=1)
+    z_in = np.kron(two, np.concatenate([line, line @ turn], axis=0))
+    y_in = np.concatenate([cosine.T, sine.T], axis=0)
     z_out = np.concatenate([np.kron(two, line.T), np.kron(two, turn @ line.T)], axis=1)
     y_out = np.concatenate([cosine, -sine], axis=1)
     x_in = np.zeros((2, own_modes, modes, bricks, own_modes, planes), np.float32)
@@ -73,22 +73,32 @@
     return jnp.exp(-0.5 * away * away).astype(BF16)
 
 
-def forward_lines(first, second, z_in, y_in):
-    pair = jnp.concatenate([first.astype(BF16), second.astype(BF16)], axis=1)
-    both = dot(pair, z_in).astype(BF16)
-    return dot(y_in, jnp.concatenate([both[:, :128], both[:, 128:]], axis=0))
-
-
-def inverse_lines(values, z_out, y_out):
-    both = dot(values.astype(BF16), z_out).astype(BF16)
-    return dot(y_out, jnp.concatenate([both[:, :256], both[:, 256:]], axis=0))
+def forward_lines(lines_of, channels, z_in, y_in):
+    modes = y_in.shape[0] // 2
+    wide = []
+    for p in range(channels // 2):
+        pair = jnp.concatenate([lines_of(2 * p).astype(BF16), lines_of(2 * p + 1).astype(BF16)], axis=1)
+        turned = dot(y_in, pair).astype(BF16)
+        cosine, sine = turned[:modes], turned[modes:]
+        wide.append(
+            jnp.concatenate([cosine[:, :128], sine[:, :128], cosine[:, 128:], sine[:, 128:]], axis=1)
+        )
+    return dot(jnp.concatenate(wide, axis=0), z_in)
+
+
+def inverse_lines(values_of, channels, modes, z_out, y_out):
+    values = jnp.concatenate([values_of(p).astype(BF16) for p in range(channels // 2)], axis=0)
+    both = dot(values, z_out).astype(BF16)
+    for p in range(channels // 2):
+        rows = both[p * modes : (p + 1) * modes]
+        yield p, dot(y_out, jnp.concatenate([rows[:, :256], rows[:, 256:]], axis=0))
 
 
 def encode_kernel(capacity, planes, grid, base, got, z_in, y_in, encoded, y_modes, total, held):
     x = pl.program_id(0)
     channels = got.shape[1] - 8
     pitch = channels + 8
-    modes = y_in.shape[0]
+    modes = y_in.shape[0] // 2
     exchange_rows = modes * planes
 
     @pl.when(x == 0)
@@ -124,14 +134,13 @@
             pl.ds(start + y * pitch, channels), :
         ].astype(BF16)
 
+    out = forward_lines(
+        lambda c: total[pl.ds(start + c, grid, stride=pitch), :], channels, z_in[...], y_in[...]
+    )
     for p in range(channels // 2):
-        out = forward_lines(
-            total[pl.ds(start + 2 * p, grid, stride=pitch), :],
-            total[pl.ds(start + 2 * p + 1, grid, stride=pitch), :],
-            z_in[...],
-            y_in[...],
-        )
-        held[pl.ds(p * exchange_rows + x, modes, stride=planes), :] = out
+        held[pl.ds(p * exchange_rows + x, modes, stride=planes), :] = out[
+            p * modes : (p + 1) * modes
+        ]
 
     @pl.when(x == planes - 1)
     def _():
@@ -233,7 +242,7 @@
     x = pl.program_id(0)
     channels, grid = cotangent.shape[0], cotangent.shape[2]
     pitch = channels + 8
-    modes = y_in.shape[0]
+    modes = y_in.shape[0] // 2
     exchange_rows = modes * planes
 
     @pl.when(x == 0)
@@ -248,15 +257,16 @@
 
     root = math.sqrt(2.0 / math.pi)
 
-    for p in range(channels // 2):
-        values = held[pl.ds(p * exchange_rows + x, modes, stride=planes), :]
-        spectral = inverse_lines(values, z_out[...], y_out[...])
+    def values_of(p):
+        return held[pl.ds(p * exchange_rows + x, modes, stride=planes), :]
+
+    for p, spectral in inverse_lines(values_of, channels, modes, z_out[...], y_out[...]):
         for h in range(2):
             d = 2 * p + h
             mixed = skipped[pl.ds(d, grid, stride=pitch), :]
             pre_act[d] = spectral[:, h * 128 : (h + 1) * 128] + mixed
 
-    @pl.loop(0, channels, unroll=2)
+    @pl.loop(0, channels, unroll=32)
     def _(d):
         pre = pre_act[d]
         square = pre * pre
@@ -268,13 +278,13 @@
         )
         grads[pl.ds(d, grid, stride=pitch), :] = cotangent[d, 0].astype(F32) * slope
 
+    out = forward_lines(
+        lambda c: grads[pl.ds(c, grid, stride=pitch), :], channels, z_in[...], y_in[...]
+    )
     for p in range(channels // 2):
-        held_out[pl.ds(p * exchange_rows + x, modes, stride=planes), :] = forward_lines(
-            grads[pl.ds(2 * p, grid, stride=pitch), :],
-            grads[pl.ds(2 * p + 1, grid, stride=pitch), :],
-            z_in[...],
-            y_in[...],
-        )
+        held_out[pl.ds(p * exchange_rows + x, modes, stride=planes), :] = out[
+            p * modes : (p + 1) * modes
+        ]
 
     for y in range(grid):
         grad_rows[y * channels : (y + 1) * channels, :] = grads[
@@ -317,9 +327,10 @@
 
     @pl.loop(0, planes)
     def _(x):
-        for p in range(channels // 2):
-            values = held[pl.ds(p * exchange_rows + x, modes, stride=planes), :]
-            lines = inverse_lines(values, z_out[...], y_out[...])
+        def values_of(p):
+            return held[pl.ds(p * exchange_rows + x, modes, stride=planes), :]
+
+        for p, lines in inverse_lines(values_of, channels, modes, z_out[...], y_out[...]):
             for h in range(2):
                 start = x * (grid * pitch) + 2 * p + h
                 total[pl.ds(start, grid, stride=pitch), :] = lines[:, h * 128 : (h + 1) * 128]

time: 288 us -> 264 us (0.917)
  Pallas kernels: 95.2 us -> 71.3 us
    pallas_call x1, Pallas kernels: 41.9 us -> 30 us  [shards(): pl.pallas_call(lambda *refs: layer_kernel(planes, *refs), grid=(planes,),...]
    pallas_call x1, Pallas kernels: 25.7 us -> 16.2 us  [shards(): pl.pallas_call(lambda *refs: encode_kernel(capacity, planes, grid, *refs)...]
  transfers between devices with their start and end apart: 4 -> 4, of which waited for: 4 -> 4; matrix products, arithmetic and copies ran while one was open for 5% -> 6% of each run, Pallas kernels for 0% -> 0%
where the time goes in v4:
time: 264 us; the launch traced here: 263 us
  waiting for transfers between devices  77.4 us (29%)
  Pallas kernels  71.3 us (27%)
  blocking collectives  60.8 us (23%)
  starting transfers between devices  24.4 us (9%)
  local copies, waits for them, and re-layouts  21.4 us (8%)
  other arithmetic  6.14 us (2%)
    all_to_all x4, waiting for transfers between devices, exchange(): lax.all_to_all(values, 'brick', split_axis=0, concat_axis=0, tiled=True)  77.4 us
    all_to_all x2, blocking collectives, exchange(): lax.all_to_all(values, 'brick', split_axis=0, concat_axis=0, tiled=True)  60.8 us
    pallas_call x1, Pallas kernels, shards(): pl.pallas_call(lambda *refs: layer_kernel(planes, *refs), grid=(planes,),...  30 us
    all_to_all x4, starting transfers between devices, exchange(): lax.all_to_all(values, 'brick', split_axis=0, concat_axis=0, tiled=True)  24.4 us
    pallas_call x1, Pallas kernels, shards(): pl.pallas_call(lambda *refs: encode_kernel(capacity, planes, grid, *refs)...  16.2 us
    pallas_call x1, Pallas kernels, shards(): pl.pallas_call(lambda *refs: pull_kernel(capacity, planes, grid, *refs),...  13.4 us
    pallas_call x1, Pallas kernels, shards(): pl.pallas_call(middle_grad_kernel, in_specs=[vmem()] * 6, out_specs=[vmem...  6.22 us
    unnamed x19, local copies, waits for them, and re-layouts  6.03 us
  transfers between devices with their start and end apart: 4, of which 4 were waited for; matrix products, arithmetic and copies ran while one was open for 6% of the time, Pallas kernels for 0%

profile of v4, /device:TPU:1, one launch (start us, length us, event | category | flops | bytes accessed | tf_op | source)
XLA Modules:
  0.0 263.3 jit_solution(15122315134059936393)
XLA Ops:
  0.7 0.8 fusion.10
  1.5 0.8 select_reduce_fusion
  2.4 1.0 fusion.23
  3.4 1.0 copy.123
  4.4 0.7 reduce_min.9
  5.1 0.7 add_convert_fusion
  5.8 0.1 constant_dynamic-update-slice_fusion.7
  5.9 0.1 constant_dynamic-update-slice_fusion.6
  5.9 0.1 constant_dynamic-update-slice_fusion.5
  6.0 0.1 constant_dynamic-update-slice_fusion.4
  6.1 0.1 constant_dynamic-update-slice_fusion
  6.2 0.5 fusion.13
  6.8 0.4 copy.129
  7.2 31.2 %all_to_all.54.refs_1_ = bf16[96,40,128]{2,1,0:T(8,128)(2,1)S(1)} all-to-all(bf16[96,40,128]{2,1,0:T(8,128)(2,1)S(1)} %copy.129), channel_id=1, replica_groups=mesh['groups'=2,'brick'=16] {'brick'}, dimensions={0} | all-to-all | bytes 1966080 | tf_op jit(solution)/shard_map/all_to_all | solution.py:385
  38.4 0.8 fusion.2.refs_0_
  39.2 0.1 copy-done
  39.3 16.2 %encode.1 = (bf16[32768,128]{1,0:T(8,128)(2,1)}, bf16[256,2048]{1,0:T(8,128)(2,1)}) custom-call(s32[96]{0:T(128)} %fusion.2.refs_0_, bf16[96,40,128]{2,1,0:T(8,128)(2,1)} %copy-done, bf16[512,128]{1,0:T(8,128)(2,1)} %constant.67.clone.refs_2_, bf16[64,128]{1,0:T(8,128)(2,1)} %constant.68.clone.refs_3_.refs_7_), custom_call_target="tpu_custom_call" | custom-call | tf_op jit(solution)/shard_map/encode/pallas_call | solution.py:446
  55.5 4.4 %all-to-all-start.1 = ((bf16[16,16,2048]{2,1,0:T(8,128)(2,1)}), bf16[16,16,2048]{2,1,0:T(8,128)(2,1)S(1)}, u32[]{:S(2)}, u32[]{:S(2)}) async-start(bf16[16,16,2048]{2,1,0:T(8,128)(2,1)} %bitcast.77), calls=%async_computation.1 | async-start | bytes 2097152 | tf_op jit(solution)/shard_map/all_to_all | solution.py:385
  59.9 0.2 reshape.347
  60.1 0.3 slice_reduce_fusion.11
  60.4 0.1 copy.115
  60.5 0.3 copy.116
  60.8 0.6 broadcast_in_dim.50
  61.4 1.0 reshape.349.weights
  62.5 0.6 copy.114
  63.1 1.2 reshape.346.scale
  64.2 18.8 %all-to-all-done.1 = bf16[16,16,2048]{2,1,0:T(8,128)(2,1)S(1)} async-done(((bf16[16,16,2048]{2,1,0:T(8,128)(2,1)}), bf16[16,16,2048]{2,1,0:T(8,128)(2,1)S(1)}, u32[]{:S(2)}, u32[]{:S(2)}) %all-to-all-start.1) | async-done | bytes 1048608 | tf_op jit(solution)/shard_map/all_to_all | solution.py:385
  83.0 1.0 copy-done.3
  84.0 5.5 %middle.1 = (f32[64,2048]{1,0:T(8,128)}, bf16[256,2048]{1,0:T(8,128)(2,1)}) custom-call(bf16[256,2048]{1,0:T(8,128)(2,1)} %bitcast.69, bf16[128,256]{1,0:T(8,128)(2,1)} %constant.69.clone.x_in, bf16[256,128]{1,0:T(8,128)(2,1)} %constant.70.clone.x_out, f32[64,2048]{1,0:T(8,128)} %reshape.346.scale, f32[16,32,128]{2,1,0:T(8,128)} %reshape.349.weights), custom_call_target="tpu_custom_call" | custom-call | tf_op jit(solution)/shard_map/middle/pallas_call | solution.py:468
  89.5 6.7 %all-to-all-start.2 = ((bf16[16,16,2048]{2,1,0:T(8,128)(2,1)}), bf16[16,16,2048]{2,1,0:T(8,128)(2,1)S(1)}, u32[]{:S(2)}, u32[]{:S(2)}) async-start(bf16[16,16,2048]{2,1,0:T(8,128)(2,1)} %bitcast.78), calls=%async_computation.2 | async-start | bytes 2097152 | tf_op jit(solution)/shard_map/all_to_all | solution.py:385
  96.2 0.1 broadcast_multiply_fusion
  96.4 1.0 mul.80.refs_3_
  97.4 22.0 %all-to-all-done.2 = bf16[16,16,2048]{2,1,0:T(8,128)(2,1)S(1)} async-done(((bf16[16,16,2048]{2,1,0:T(8,128)(2,1)}), bf16[16,16,2048]{2,1,0:T(8,128)(2,1)S(1)}, u32[]{:S(2)}, u32[]{:S(2)}) %all-to-all-start.2) | async-done | bytes 1048608 | tf_op jit(solution)/shard_map/all_to_all | solution.py:385
  119.4 1.0 copy-done.4
  120.4 30.0 %layer.1 = (bf16[32,8,128,128]{3,2,1,0:T(8,128)(2,1)}, bf16[32768,128]{1,0:T(8,128)(2,1)}, bf16[256,2048]{1,0:T(8,128)(2,1)}) custom-call(bf16[256,2048]{1,0:T(8,128)(2,1)} %bitcast.70, bf16[32768,128]{1,0:T(8,128)(2,1)} %get-tuple-element.14.refs_1_, bf16[32,8,128,128]{3,2,1,0:T(8,128)(2,1)} %refs_2_.2, bf16[256,256]{1,0:T(8,128)(2,1)} %mul.80.refs_3_, ...), custom_call_target="tpu_custom_call" | custom-call | tf_op jit(solution)/shard_map/layer/pallas_call | solution.py:485
  150.3 6.7 %all-to-all-start.3 = ((bf16[16,16,2048]{2,1,0:T(8,128)(2,1)}), bf16[16,16,2048]{2,1,0:T(8,128)(2,1)S(1)}, u32[]{:S(2)}, u32[]{:S(2)}) async-start(bf16[16,16,2048]{2,1,0:T(8,128)(2,1)} %bitcast.76), calls=%async_computation.3 | async-start | bytes 2097152 | tf_op jit(solution)/shard_map/all_to_all | solution.py:385
  157.0 0.1 copy.117
  157.1 0.2 reshape.350
  157.2 0.3 slice_reduce_fusion.7
  157.6 0.1 copy.118
  157.6 0.3 copy.119
  158.0 0.6 broadcast_in_dim.51
  158.6 1.0 reshape.352.weights
  159.6 20.5 %all-to-all-done.3 = bf16[16,16,2048]{2,1,0:T(8,128)(2,1)S(1)} async-done(((bf16[16,16,2048]{2,1,0:T(8,128)(2,1)}), bf16[16,16,2048]{2,1,0:T(8,128)(2,1)S(1)}, u32[]{:S(2)}, u32[]{:S(2)}) %all-to-all-start.3) | async-done | bytes 1048608 | tf_op jit(solution)/shard_map/all_to_all | solution.py:385
  180.1 1.1 copy-done.2
  181.2 6.2 %middle_grad.1 = (bf16[256,2048]{1,0:T(8,128)(2,1)}, f32[512,128]{1,0:T(8,128)}) custom-call(bf16[256,2048]{1,0:T(8,128)(2,1)} %bitcast.68, bf16[128,256]{1,0:T(8,128)(2,1)} %constant.69.clone.x_in, bf16[256,128]{1,0:T(8,128)(2,1)} %constant.70.clone.x_out, f32[64,2048]{1,0:T(8,128)} %reshape.346.scale, f32[16,32,128]{2,1,0:T(8,128)} %reshape.352.weights, ...), custom_call_target="tpu_custom_call" | custom-call | tf_op jit(solution)/shard_map/middle_grad/pallas_call | solution.py:524
  187.4 6.7 %all-to-all-start.4 = ((bf16[16,16,2048]{2,1,0:T(8,128)(2,1)}), bf16[16,16,2048]{2,1,0:T(8,128)(2,1)S(1)}, u32[]{:S(2)}, u32[]{:S(2)}) async-start(bf16[16,16,2048]{2,1,0:T(8,128)(2,1)} %bitcast.75), calls=%async_computation.4 | async-start | bytes 2097152 | tf_op jit(solution)/shard_map/all_to_all | solution.py:385
  194.1 0.1 copy.120
  194.2 0.1 broadcast_multiply_fusion.1
  194.3 0.7 mul.84.refs_4_
  195.1 1.3 reshape.353
  196.3 0.8 reduce_sum.35
  197.2 2.8 %slice_reduce_fusion.3 = (f32[16,16]{1,0:T(8,128)S(1)}, f32[16,16]{1,0:T(8,128)S(1)}, f32[16,16]{1,0:T(8,128)S(1)}, f32[16,16]{1,0:T(8,128)S(1)}) fusion(f32[16,16,2,2]{3,2,1,0:T(2,128)S(1)} %reduce_sum.35), kind=kLoop, calls=%fused_computation.10 | loop fusion | bytes 8192 | tf_op jit(solution)/shard_map/slice | solution.py:546
  200.0 0.3 copy.121
  200.3 0.2 reshape_reshape.3
  200.5 0.6 fusion.16.refs_7_
  201.1 16.1 %all-to-all-done.4 = bf16[16,16,2048]{2,1,0:T(8,128)(2,1)S(1)} async-done(((bf16[16,16,2048]{2,1,0:T(8,128)(2,1)}), bf16[16,16,2048]{2,1,0:T(8,128)(2,1)S(1)}, u32[]{:S(2)}, u32[]{:S(2)}) %all-to-all-start.4) | async-done | bytes 1048608 | tf_op jit(solution)/shard_map/all_to_all | solution.py:385
  217.2 1.1 copy-done.1
  218.3 13.4 %pull.1 = bf16[112,32,128]{2,1,0:T(8,128)(2,1)} custom-call(s32[96]{0:T(128)} %fusion.2.refs_0_, bf16[96,40,128]{2,1,0:T(8,128)(2,1)} %copy-done, bf16[256,2048]{1,0:T(8,128)(2,1)} %bitcast.67, bf16[32768,128]{1,0:T(8,128)(2,1)} %get-tuple-element.19.refs_3_, bf16[128,128]{1,0:T(8,128)(2,1)} %mul.84.refs_4_, bf16[128,512]{1,0:T(8,128)(2,1)} %constant.74.clone.refs_5_, ...), custom_call_target="tpu_custom_call" | custom-call | tf_op jit(solution)/shard_map/pull/pallas_call | solution.py:560
  231.8 29.6 %all_to_all.55 = bf16[112,32,128]{2,1,0:T(8,128)(2,1)S(1)} all-to-all(bf16[112,32,128]{2,1,0:T(8,128)(2,1)} %pull.1), channel_id=1, replica_groups=mesh['groups'=2,'brick'=16] {'brick'}, dimensions={0} | all-to-all | bytes 1835008 | tf_op jit(solution)/shard_map/all_to_all | solution.py:385
  261.4 0.1 slice.99
  261.5 0.3 convolution_convert_fusion
  261.8 0.8 copy.130
  262.6 0.7 div.26
  (31 shorter events, 0.3 us)
Async XLA Ops:
  0.6 59.3 %copy-start.6 = (f32[32,32]{1,0:T(8,128)S(1)}, f32[32,32]{1,0:T(8,128)}, u32[]{:S(2)}) copy-start(f32[32,32]{1,0:T(8,128)} %param.25) | copy-start | bytes 12292
  0.6 61.8 %copy-start.5 = (f32[32,32,2,64]{3,2,1,0:T(2,128)S(1)}, f32[32,32,2,64]{3,2,1,0:T(2,128)}, u32[]{:S(2)}) copy-start(f32[32,32,2,64]{3,2,1,0:T(2,128)} %param.24) | copy-start | bytes 1572868
  7.1 89.1 %copy-start.7 = (bf16[32,32]{1,0:T(8,128)(2,1)S(1)}, bf16[32,32]{1,0:T(8,128)(2,1)}, u32[]{:S(2)}) copy-start(bf16[32,32]{1,0:T(8,128)(2,1)} %param.26) | copy-start | bytes 6148
  38.4 1.0 copy-start
  55.5 27.5 %all-to-all-start.1 = ((bf16[16,16,2048]{2,1,0:T(8,128)(2,1)}), bf16[16,16,2048]{2,1,0:T(8,128)(2,1)S(1)}, u32[]{:S(2)}, u32[]{:S(2)}) async-start(bf16[16,16,2048]{2,1,0:T(8,128)(2,1)} %bitcast.77), calls=%async_computation.1 | async-start | bytes 2097152 | tf_op jit(solution)/shard_map/all_to_all | solution.py:385
  83.0 1.0 copy-start.3
  89.5 29.8 %all-to-all-start.2 = ((bf16[16,16,2048]{2,1,0:T(8,128)(2,1)}), bf16[16,16,2048]{2,1,0:T(8,128)(2,1)S(1)}, u32[]{:S(2)}, u32[]{:S(2)}) async-start(bf16[16,16,2048]{2,1,0:T(8,128)(2,1)} %bitcast.78), calls=%async_computation.2 | async-start | bytes 2097152 | tf_op jit(solution)/shard_map/all_to_all | solution.py:385
  119.4 1.0 copy-start.4
  150.3 29.8 %all-to-all-start.3 = ((bf16[16,16,2048]{2,1,0:T(8,128)(2,1)}), bf16[16,16,2048]{2,1,0:T(8,128)(2,1)S(1)}, u32[]{:S(2)}, u32[]{:S(2)}) async-start(bf16[16,16,2048]{2,1,0:T(8,128)(2,1)} %bitcast.76), calls=%async_computation.3 | async-start | bytes 2097152 | tf_op jit(solution)/shard_map/all_to_all | solution.py:385
  180.1 1.1 copy-start.2
  187.4 29.8 %all-to-all-start.4 = ((bf16[16,16,2048]{2,1,0:T(8,128)(2,1)}), bf16[16,16,2048]{2,1,0:T(8,128)(2,1)S(1)}, u32[]{:S(2)}, u32[]{:S(2)}) async-start(bf16[16,16,2048]{2,1,0:T(8,128)(2,1)} %bitcast.75), calls=%async_computation.4 | async-start | bytes 2097152 | tf_op jit(solution)/shard_map/all_to_all | solution.py:385
  217.2 1.1 copy-start.1
